TPU v7x, 32 devices: a whole 2x2x4 slice. The times are simulated.
32 devices in a mesh: rows: 4 (over x, core), chan: 8 (over z, y).
Axes of the slice: x: 2, y: 2, z: 4, core: 2. Of those that a mesh axis runs over, the one named last changes fastest.
Arguments:
- inputs: bfloat16 [8192, 1024], P(('rows', 'chan')), may hold values from -6 to 6
- mix_gain: float32 [1024], replicated, may hold values from 0.5 to 1.5
- gate_proj: bfloat16 [1024, 1536], P(None, 'chan'), may hold values from -0.1875 to 0.1875
- gate_bias: float32 [1536], replicated, may hold values from -3 to 3
- lift_proj: bfloat16 [1024, 1536], P(None, 'chan'), may hold values from -0.1875 to 0.1875
- lift_bias: float32 [1536], replicated, may hold values from -3 to 3
- conv_taps: float32 [4, 1536], replicated, may hold values from -3 to 3
- conv_bias: float32 [1536], replicated, may hold values from -2 to 2
- recur_gate: float32 [8, 192, 192], replicated, may hold values from -0.4375 to 0.4375
- recur_bias: float32 [1536], replicated, may hold values from -3 to 3
- input_gate: float32 [8, 192, 192], replicated, may hold values from -0.4375 to 0.4375
- input_bias: float32 [1536], replicated, may hold values from -3 to 3
- decay_param: float32 [1536], replicated, may hold values from 2.2 to 6.9
- out_proj: bfloat16 [1536, 1024], P('chan'), may hold values from -0.15625 to 0.15625
- out_bias: float32 [1024], replicated, may hold values from -2 to 2
- mlp_gain: float32 [1024], replicated, may hold values from 0.5 to 1.5
- mlp_gate: bfloat16 [1024, 3072], P(None, 'chan'), may hold values from -0.1875 to 0.1875
- mlp_up: bfloat16 [1024, 3072], P(None, 'chan'), may hold values from -0.1875 to 0.1875
- mlp_down: bfloat16 [3072, 1024], P('chan'), may hold values from -0.109375 to 0.109375
- doc_starts: int32 [4, 8], P('rows'), may hold values from 0 to 2048, as said below
- cotangent: bfloat16 [8192, 1024], P(('rows', 'chan')), may hold values from -6 to 6
Outputs:
- output: bfloat16 [8192, 1024], P(('rows', 'chan'))
- grad_inputs: bfloat16 [8192, 1024], P(('rows', 'chan'))
- grad_mix_gain: float32 [1024], P('chan')
- grad_gate_proj: float32 [1024, 1536], P(None, 'chan')
- grad_gate_bias: float32 [1536], P('chan')
- grad_lift_proj: float32 [1024, 1536], P(None, 'chan')
- grad_lift_bias: float32 [1536], P('chan')
- grad_conv_taps: float32 [4, 1536], P(None, 'chan')
- grad_conv_bias: float32 [1536], P('chan')
- grad_recur_gate: float32 [8, 192, 192], P(None, 'chan')
- grad_recur_bias: float32 [1536], P('chan')
- grad_input_gate: float32 [8, 192, 192], P(None, 'chan')
- grad_input_bias: float32 [1536], P('chan')
- grad_decay_param: float32 [1536], P('chan')
- grad_out_proj: float32 [1536, 1024], P('chan')
- grad_out_bias: float32 [1024], P('chan')
- grad_mlp_gain: float32 [1024], P('chan')
- grad_mlp_gate: float32 [1024, 3072], P(None, 'chan')
- grad_mlp_up: float32 [1024, 3072], P(None, 'chan')
- grad_mlp_down: float32 [3072, 1024], P('chan')
Inputs may be any that keep to these rules, and one draw needn't show every extreme that they name: `doc_starts`: each row is non-decreasing, begins with 0 and ends with 2048; entries equal to 2048 mark no document and stand only at the row's end.
All inputs are finite; a program needn't handle non-finite values.
Results may differ from a plain program's by a relative error of at most 0.0085.
Values may be sent and summed in bfloat16 or wider, within the bound.
A program may use at most 320 MiB of HBM per device.

v0:
```python
from functools import partial
import math

import jax
import jax.numpy as jnp
from jax import lax
from jax.sharding import PartitionSpec as P

D = 1024
LRU = 1536
FF = 3072
HEADS = 8
GB = 192


EPSILON = 1e-06
precise = lax.Precision.HIGHEST


def from_behind(block, axis, distance):
    devices = range(lax.axis_size(axis))
    route = [(i - distance, i) for i in devices if i - distance in devices]
    return lax.ppermute(block, axis, route)


def prefix(value, axis, join, neutral, backward):
    count, mine = (lax.axis_size(axis), lax.axis_index(axis))
    pieces = jax.tree.map(lambda part: lax.all_gather(part, axis), value)
    if backward:
        pieces = jax.tree.map(lambda part: part[::-1], pieces)
        mine = count - 1 - mine
    subtotal = jax.tree.map(
        lambda part, zero: jnp.full_like(part, 0) + jnp.asarray(zero, part.dtype), value, neutral
    )

    def hop(position, subtotal):
        longer = join(subtotal, jax.tree.map(lambda part: part[position], pieces))
        return jax.tree.map(lambda new, old: jnp.where(position < mine, new, old), longer, subtotal)

    return lax.fori_loop(0, count - 1, hop, subtotal)


def rms_scale(values, gain_vec):
    return (
        values * lax.rsqrt(jnp.mean(values * values, axis=-1, keepdims=True) + EPSILON) * gain_vec
    )


def gated_unit(gate_pre, up_vals):
    return jax.nn.gelu(gate_pre) * up_vals


def affine(earlier, later_map):
    return (earlier[0] * later_map[0], later_map[0] * earlier[1] + later_map[1])


def segment_ids(starts, start_pos, pos_count, seq_len):
    where_at = start_pos + jnp.arange(pos_count, dtype=jnp.int32)
    seq_of = jnp.floor_divide(where_at, seq_len)
    within = where_at - seq_of * seq_len
    owner = seq_of[:, None] == jnp.arange(starts.shape[0], dtype=jnp.int32)[None, :]
    passed = starts[None, :, :] <= within[:, None, None]
    doc_tally = jnp.sum(jnp.logical_and(owner[:, :, None], passed).astype(jnp.int32), axis=(1, 2))
    return seq_of * (starts.shape[1] + 1) + doc_tally


def project(normed, weights, first_bias, second_bias):
    product = jnp.einsum("td,dc->ct", normed, weights, preferred_element_type=jnp.float32)
    channels = first_bias.shape[0]
    return (product[:channels] + first_bias[:, None], product[channels:] + second_bias[:, None])


def conv_forward(lifted, tail_rows, segments, tap_vals, bias_vec):
    length = lifted.shape[1]
    extended = jnp.concatenate([tail_rows, lifted], axis=1)
    own_seg = segments[3 : 3 + length]
    result = bias_vec[:, None] + tap_vals[0][:, None] * lifted
    for offset in range(1, 4):
        same_doc = (segments[3 - offset : 3 - offset + length] == own_seg).astype(jnp.float32)
        result = (
            result
            + tap_vals[offset][:, None]
            * extended[:, 3 - offset : 3 - offset + length]
            * same_doc[None, :]
        )
    return result


def conv_backward(grad_conv, head_rows, segments, lifted, tail_rows, tap_vals):
    length = grad_conv.shape[1]
    ahead_grad = jnp.concatenate([grad_conv, head_rows], axis=1)
    behind = jnp.concatenate([tail_rows, lifted], axis=1)
    own_seg = segments[3 : 3 + length]
    grad_lifted = tap_vals[0][:, None] * grad_conv
    tap_grads = [jnp.sum(grad_conv * lifted, axis=1)]
    for offset in range(1, 4):
        later_same = (segments[3 + offset : 3 + offset + length] == own_seg).astype(jnp.float32)
        grad_lifted = (
            grad_lifted
            + tap_vals[offset][:, None]
            * ahead_grad[:, offset : offset + length]
            * later_same[None, :]
        )
        earlier = (segments[3 - offset : 3 - offset + length] == own_seg).astype(jnp.float32)
        tap_grads.append(
            jnp.sum(
                grad_conv * behind[:, 3 - offset : 3 - offset + length] * earlier[None, :], axis=1
            )
        )
    return (grad_lifted, jnp.stack(tap_grads, axis=1), jnp.sum(grad_conv, axis=1))


def coefficients(is_reset, conv_out, recur_gate, recur_bias, input_gate, input_bias, decay_param):
    channels, length = conv_out.shape
    gate_block = recur_gate.shape[1]
    grouped = conv_out.reshape(channels // gate_block, gate_block, length)
    recurrence = jax.nn.sigmoid(
        jnp.einsum("hit,hio->hot", grouped, recur_gate, precision=precise).reshape(channels, length)
        + recur_bias[:, None]
    )
    opening = jax.nn.sigmoid(
        jnp.einsum("hit,hio->hot", grouped, input_gate, precision=precise).reshape(channels, length)
        + input_bias[:, None]
    )
    log_decay = -8.0 * recurrence * jax.nn.softplus(-decay_param)[:, None]
    decay_rate = jnp.where(is_reset[None, :], 0.0, jnp.exp(log_decay))
    scaling = jnp.where(is_reset[None, :], 1.0, jnp.sqrt(-jnp.expm1(2.0 * log_decay)))
    return (decay_rate, scaling * opening * conv_out)


def reverse_local(decay_rate, grad_state):
    ones_col = jnp.ones_like(decay_rate[:, :1])
    factor = jnp.flip(jnp.concatenate([decay_rate[:, 1:], ones_col], axis=1), axis=1)
    product, carried = lax.associative_scan(affine, (factor, jnp.flip(grad_state, axis=1)), axis=1)
    return (jnp.flip(product, axis=1), jnp.flip(carried, axis=1))


def finish_state(lru_state, start_state, carried, pull_coef):
    previous = jnp.concatenate([start_state[:, None], lru_state[:, :-1]], axis=1)
    return pull_coef((carried * previous, carried))


def flatten_rows(pieces, row_count):
    return jnp.concatenate([source.reshape(row_count, -1) for source in pieces], axis=1)


def body(
    inputs,
    mix_gain,
    gate_proj,
    gate_bias,
    lift_proj,
    lift_bias,
    conv_taps,
    conv_bias,
    recur_gate,
    recur_bias,
    input_gate,
    input_bias,
    decay_param,
    out_proj,
    out_bias,
    mlp_gain,
    mlp_gate,
    mlp_up,
    mlp_down,
    doc_starts,
    cotangent,
):
    chan_count = lax.axis_size("chan")
    chan_place = lax.axis_index("chan")
    local_rows = inputs.shape[0]
    seq_length = local_rows * chan_count
    rows_f32 = inputs.astype(jnp.float32)
    cot_f32 = cotangent.astype(jnp.float32)
    normed, pull_norm = jax.vjp(rms_scale, rows_f32, mix_gain)
    normed_low = normed.astype(jnp.bfloat16)
    gate_full, lift_full, out_full, mlp_gate_full, mlp_up_full, mlp_down_full = (
        lax.all_gather(gate_proj, "chan", axis=1, tiled=True),
        lax.all_gather(lift_proj, "chan", axis=1, tiled=True),
        lax.all_gather(out_proj, "chan", axis=0, tiled=True),
        lax.all_gather(mlp_gate, "chan", axis=1, tiled=True),
        lax.all_gather(mlp_up, "chan", axis=1, tiled=True),
        lax.all_gather(mlp_down, "chan", axis=0, tiled=True),
    )
    channels = LRU
    hidden_cut = FF
    segments = segment_ids(doc_starts, chan_place * local_rows - 3, local_rows + 6, seq_length)
    mix_proj = jnp.concatenate([gate_full, lift_full], axis=1)
    gate_pre, lifted = project(normed_low, mix_proj, gate_bias, lift_bias)
    tail_rows = from_behind(lifted[:, -3:], "chan", 1)
    conv_out = conv_forward(lifted, tail_rows, segments, conv_taps, conv_bias)
    is_reset = segments[3 : 3 + local_rows] != segments[2 : 2 + local_rows]
    (decay_rate, lru_input), pull_coef = jax.vjp(
        partial(coefficients, is_reset),
        conv_out,
        recur_gate,
        recur_bias,
        input_gate,
        input_bias,
        decay_param,
    )
    running, local_state = lax.associative_scan(affine, (decay_rate, lru_input), axis=1)
    ones_vec = jnp.ones((channels,), jnp.float32)
    zeros_vec = jnp.zeros((channels,), jnp.float32)
    _, start_state = prefix(
        (running[:, -1], local_state[:, -1]), "chan", affine, (ones_vec, zeros_vec), False
    )
    lru_state = local_state + running * start_state[:, None]
    gate_val, pull_gelu = jax.vjp(jax.nn.gelu, gate_pre)
    mixed_out = (lru_state * gate_val).astype(jnp.bfloat16)
    resid = (
        rows_f32
        + jnp.einsum("ct,cd->td", mixed_out, out_full, preferred_element_type=jnp.float32)
        + out_bias
    )
    normed2, pull_norm2 = jax.vjp(rms_scale, resid, mlp_gain)
    normed2_low = normed2.astype(jnp.bfloat16)
    mlp_proj = jnp.concatenate([mlp_gate_full, mlp_up_full], axis=1)
    mlp_pre = jnp.einsum("td,df->ft", normed2_low, mlp_proj, preferred_element_type=jnp.float32)
    hidden, pull_mlp = jax.vjp(gated_unit, mlp_pre[:hidden_cut], mlp_pre[hidden_cut:])
    hidden_low = hidden.astype(jnp.bfloat16)
    output = (
        resid
        + jnp.einsum("ft,fd->td", hidden_low, mlp_down_full, preferred_element_type=jnp.float32)
    ).astype(jnp.bfloat16)
    grad_down = jnp.einsum("ft,td->fd", hidden_low, cotangent, preferred_element_type=jnp.float32)
    grad_gate_m, grad_up_m = pull_mlp(
        jnp.einsum("td,fd->ft", cotangent, mlp_down_full, preferred_element_type=jnp.float32)
    )
    grad_pre = jnp.concatenate([grad_gate_m, grad_up_m], axis=0).astype(jnp.bfloat16)
    grad_mlp_in = jnp.einsum("ft,td->fd", grad_pre, normed2_low, preferred_element_type=jnp.float32)
    grad_resid_part, grad_gain2 = pull_norm2(
        jnp.einsum("ft,df->td", grad_pre, mlp_proj, preferred_element_type=jnp.float32)
    )
    grad_resid = cot_f32 + grad_resid_part
    grad_branch = grad_resid.astype(jnp.bfloat16)
    grad_out_proj = jnp.einsum(
        "ct,td->cd", mixed_out, grad_branch, preferred_element_type=jnp.float32
    )
    grad_mixed = jnp.einsum("td,cd->ct", grad_branch, out_full, preferred_element_type=jnp.float32)
    product, carried = reverse_local(decay_rate, grad_mixed * gate_val)
    _, incoming = prefix(
        (decay_rate[:, 0] * product[:, 0], decay_rate[:, 0] * carried[:, 0]),
        "chan",
        affine,
        (ones_vec, zeros_vec),
        True,
    )
    carried = carried + product * incoming[:, None]
    coef_grads = finish_state(lru_state, start_state, carried, pull_coef)
    head_rows = from_behind(coef_grads[0][:, :3], "chan", -1)
    grad_lifted, grad_taps, grad_conv_bias = conv_backward(
        coef_grads[0], head_rows, segments, lifted, tail_rows, conv_taps
    )
    (grad_gate_pre,) = pull_gelu(grad_mixed * lru_state)
    grad_front = jnp.concatenate([grad_gate_pre, grad_lifted], axis=0).astype(jnp.bfloat16)
    grad_mix_proj = jnp.einsum(
        "ct,td->cd", grad_front, normed_low, preferred_element_type=jnp.float32
    )
    grad_normed = jnp.einsum("ct,dc->td", grad_front, mix_proj, preferred_element_type=jnp.float32)
    grad_x_part, grad_gain1 = pull_norm(grad_normed)
    grad_inputs = (grad_resid + grad_x_part).astype(jnp.bfloat16)
    grad_out_bias = jnp.sum(grad_resid, axis=0)
    pieces = [
        grad_mix_proj[:channels],
        grad_mix_proj[channels:],
        jnp.sum(grad_gate_pre, axis=1),
        jnp.sum(grad_lifted, axis=1),
        grad_taps,
        grad_conv_bias,
        jnp.transpose(coef_grads[1], (1, 0, 2)),
        coef_grads[2],
        jnp.transpose(coef_grads[3], (1, 0, 2)),
        coef_grads[4],
        coef_grads[5],
        grad_out_proj,
        grad_mlp_in[:hidden_cut],
        grad_mlp_in[hidden_cut:],
        grad_down,
        grad_gain1,
        grad_out_bias,
        grad_gain2,
    ]
    spread = flatten_rows(pieces, chan_count)
    shared = lax.psum_scatter(spread, "chan", scatter_dimension=0, tiled=True)
    summed = lax.psum(shared.reshape(-1), "rows")
    channels_dev = LRU // chan_count
    hidden_dev = FF // chan_count
    width_dev = D // chan_count
    block_dev = GB // chan_count
    shapes = [
        (channels_dev, D),
        (channels_dev, D),
        (channels_dev,),
        (channels_dev,),
        (channels_dev, 4),
        (channels_dev,),
        (block_dev, HEADS, GB),
        (channels_dev,),
        (block_dev, HEADS, GB),
        (channels_dev,),
        (channels_dev,),
        (channels_dev, D),
        (hidden_dev, D),
        (hidden_dev, D),
        (hidden_dev, D),
        (width_dev,),
        (width_dev,),
        (width_dev,),
    ]
    unpacked = []
    offset = 0
    for piece_shape in shapes:
        piece_size = math.prod(piece_shape)
        unpacked.append(summed[offset : offset + piece_size].reshape(piece_shape))
        offset = offset + piece_size
    return (
        output,
        grad_inputs,
        unpacked[15],
        unpacked[0].T,
        unpacked[2],
        unpacked[1].T,
        unpacked[3],
        unpacked[4].T,
        unpacked[5],
        jnp.transpose(unpacked[6], (1, 0, 2)),
        unpacked[7],
        jnp.transpose(unpacked[8], (1, 0, 2)),
        unpacked[9],
        unpacked[10],
        unpacked[11],
        unpacked[16],
        unpacked[17],
        unpacked[12].T,
        unpacked[13].T,
        unpacked[14],
    )


def solution(mesh):
    in_specs = (
        P(("rows", "chan"), None),
        P(),
        P(None, "chan"),
        P(),
        P(None, "chan"),
        P(),
        P(),
        P(),
        P(),
        P(),
        P(),
        P(),
        P(),
        P("chan", None),
        P(),
        P(),
        P(None, "chan"),
        P(None, "chan"),
        P("chan", None),
        P("rows", None),
        P(("rows", "chan"), None),
    )
    out_specs = (
        P(("rows", "chan"), None),
        P(("rows", "chan"), None),
        P("chan"),
        P(None, "chan"),
        P("chan"),
        P(None, "chan"),
        P("chan"),
        P(None, "chan"),
        P("chan"),
        P(None, "chan", None),
        P("chan"),
        P(None, "chan", None),
        P("chan"),
        P("chan"),
        P("chan", None),
        P("chan"),
        P("chan"),
        P(None, "chan"),
        P(None, "chan"),
        P("chan", None),
    )
    return jax.shard_map(body, mesh=mesh, in_specs=in_specs, out_specs=out_specs, check_vma=False)
```

profile of v0, /device:TPU:0, one launch (start us, length us, event | category | flops | bytes accessed | tf_op | source)
XLA Modules:
  0.0 3100.0 jit_solution(2614506673698856879)
XLA Ops:
  12.3 61.1 %all-gather.11.cloned.1.call-done = bf16[1024,1536]{0,1:T(8,128)(2,1)} async-done(((bf16[1024,192]{0,1:T(8,128)(2,1)}), bf16[1024,1536]{0,1:T(8,128)(2,1)}) %all-gather.11.cloned.1.call-update) | async-done | bytes 3145744 | tf_op jit(solution)/shard_map/all_gather | solution.py:179
  77.3 57.4 %all-gather.13.cloned.1.call-done = bf16[1024,1536]{0,1:T(8,128)(2,1)} async-done(((bf16[1024,192]{0,1:T(8,128)(2,1)}), bf16[1024,1536]{0,1:T(8,128)(2,1)}) %all-gather.13.cloned.1.call-update) | async-done | bytes 3145744 | tf_op jit(solution)/shard_map/all_gather | solution.py:180
  397.9 33.4 %all-gather = f32[12288,1]{0,1:T(1,128)S(1)} all-gather(f32[1536,1]{0,1:T(1,128)S(1)} %slice_add_fusion.5), channel_id=2, replica_groups=mesh['rows'=4,'chan'=8] {'chan'}, dimensions={0}, use_global_device_ids=true | all-gather | bytes 55296 | tf_op jit(solution)/shard_map/all_gather | solution.py:28
  445.9 31.1 %all-gather.1 = f32[12288,1]{0,1:T(1,128)S(1)} all-gather(f32[1536,1]{0,1:T(1,128)S(1)} %slice_add_fusion.4), channel_id=3, replica_groups=mesh['rows'=4,'chan'=8] {'chan'}, dimensions={0}, use_global_device_ids=true | all-gather | bytes 55296 | tf_op jit(solution)/shard_map/all_gather | solution.py:28
  492.7 7.3 slice.753
  522.0 10.8 fusion.88
  532.8 9.9 fusion.6
  542.7 11.3 multiply_reduce_fusion.5
  571.8 6.9 slice.757
  727.0 6.9 slice.813
  776.4 12.8 rev.15
  789.2 12.9 rev.16
  802.1 30.9 all-gather.2
  834.0 30.7 all-gather.3
  889.4 12.6 fusion.7
  923.9 19.7 fusion.101
  969.6 11.5 reshape.384
  981.1 11.4 reshape.385
  992.6 11.7 reshape.386
  1017.7 11.8 fusion.102
  1072.3 11.1 constant_dynamic-update-slice_fusion.9
  1099.6 1747.0 %all-reduce.72.cloned.1.call-done = f32[8,1845504]{1,0:T(8,128)} async-done(((f32[8,1845504]{1,0:T(8,128)}), f32[8,1845504]{1,0:T(8,128)}) %all-reduce.72.cloned.1.call-update) | async-done | bytes 59056144
  2846.6 82.1 %dynamic-slice_reduce_fusion.4 = f32[1845504]{0:T(1024)} fusion(f32[8,1845504]{1,0:T(8,128)} %all-reduce.72.cloned.1.call-done, u32[]{:T(128)} %bitcast.26), kind=kLoop, calls=%fused_computation.6 | loop fusion | bytes 14764036 | tf_op jit(solution)/shard_map/reshape | solution.py:287
  2936.7 129.2 %all-reduce.70.cloned.1.call-done = f32[1845504]{0:T(1024)} async-done(((f32[1845504]{0:T(1024)}), f32[1845504]{0:T(1024)}) %all-reduce.70.cloned.1.call-update) | async-done | bytes 7382032 | tf_op jit(solution)/shard_map/psum | solution.py:287
  (696 shorter events, 712.9 us)
Async XLA Ops:
  7.2 145.8 %copy-start = (f32[8,192,192]{2,1,0:T(8,128)S(1)}, f32[8,192,192]{2,1,0:T(8,128)}, u32[]{:S(2)}) copy-start(f32[8,192,192]{2,1,0:T(8,128)} %param.35) | copy-start | bytes 3538948
  7.2 66.2 %all-gather.11.cloned.1.call-start = ((), (), s32[]{:S(2)}) async-start(), calls=%async_computation | async-start | bytes 3538944 | tf_op jit(solution)/shard_map/all_gather | solution.py:179
  8.0 126.7 %all-gather.13.cloned.1.call-start = ((), (), s32[]{:S(2)}) async-start(), calls=%async_computation.1 | async-start | bytes 3538944 | tf_op jit(solution)/shard_map/all_gather | solution.py:180
  8.7 497.0 %all-gather.15.cloned.1.call-start = ((), (), s32[]{:S(2)}) async-start(), calls=%async_computation.2 | async-start | bytes 3538944 | tf_op jit(solution)/shard_map/all_gather | solution.py:181
  9.5 500.5 %all-gather.17.cloned.1.call-start = ((), (), s32[]{:S(2)}) async-start(), calls=%async_computation.3 | async-start | bytes 7077888 | tf_op jit(solution)/shard_map/all_gather | solution.py:182
  10.0 505.9 %all-gather.19.cloned.1.call-start = ((), (), s32[]{:S(2)}) async-start(), calls=%async_computation.4 | async-start | bytes 7077888 | tf_op jit(solution)/shard_map/all_gather | solution.py:183
  10.6 522.2 %all-gather.21.cloned.1.call-start = ((), (), s32[]{:S(2)}) async-start(), calls=%async_computation.5 | async-start | bytes 7077888 | tf_op jit(solution)/shard_map/all_gather | solution.py:184
  11.2 2835.4 %all-reduce.72.cloned.1.call-start = ((), (), s32[]{:S(2)}) async-start(), calls=%async_computation.7 | async-start | bytes 118112256
  11.5 65.8 %copy-start.114 = (f32[256]{0:T(256)}, f32[256]{0:T(256)S(1)}, u32[]{:S(2)}) copy-start(f32[256]{0:T(256)S(1)} %fusion.43) | copy-start | bytes 3076
  11.5 127.0 %copy-start.112 = (f32[256]{0:T(256)}, f32[256]{0:T(256)S(1)}, u32[]{:S(2)}) copy-start(f32[256]{0:T(256)S(1)} %fusion.82) | copy-start | bytes 3076
  12.3 136.6 %copy-start.106 = (f32[256]{0:T(256)}, f32[256]{0:T(256)S(1)}, u32[]{:S(2)}) copy-start(f32[256]{0:T(256)S(1)} %get-tuple-element.463) | copy-start | bytes 3076
  12.3 136.6 %copy-start.108 = (f32[256]{0:T(256)}, f32[256]{0:T(256)S(1)}, u32[]{:S(2)}) copy-start(f32[256]{0:T(256)S(1)} %get-tuple-element.464) | copy-start | bytes 3076
  12.3 136.6 %copy-start.110 = (f32[256]{0:T(256)}, f32[256]{0:T(256)S(1)}, u32[]{:S(2)}) copy-start(f32[256]{0:T(256)S(1)} %get-tuple-element.466) | copy-start | bytes 3076
  12.3 156.1 %copy-start.102 = (pred[256]{0:T(512)(128)(4,1)}, pred[256]{0:T(512)(128)(4,1)S(1)}, u32[]{:S(2)}) copy-start(pred[256]{0:T(512)(128)(4,1)S(1)} %get-tuple-element.465) | copy-start | bytes 772
  12.3 156.1 %copy-start.61 = (f32[1536]{0:T(1024)}, f32[1536]{0:T(1024)S(1)}, u32[]{:S(2)}) copy-start(f32[1536]{0:T(1024)S(1)} %broadcast_multiply_fusion) | copy-start | bytes 18436
  77.3 61.2 %copy-start.99 = (f32[1024]{0:T(1024)S(1)}, f32[1024]{0:T(1024)}, u32[]{:S(2)}) copy-start(f32[1024]{0:T(1024)} %param.26) | copy-start | bytes 12292
  144.9 4.0 collective-permute-start
  789.2 77.1 %copy-start.62 = (f32[1536]{0:T(1024)S(1)}, f32[1536]{0:T(1024)}, u32[]{:S(2)}) copy-start(f32[1536]{0:T(1024)} %copy-done.61) | copy-start | bytes 18436
  789.2 77.1 %copy-start.69 = (f32[1536]{0:T(1024)S(1)}, f32[1536]{0:T(1024)}, u32[]{:S(2)}) copy-start(f32[1536]{0:T(1024)} %param.36) | copy-start | bytes 18436
  789.2 77.1 %copy-start.71 = (f32[1536]{0:T(1024)S(1)}, f32[1536]{0:T(1024)}, u32[]{:S(2)}) copy-start(f32[1536]{0:T(1024)} %param.34) | copy-start | bytes 18436
  789.2 77.1 %copy-start.88 = (f32[1536,1]{0,1:T(1,128)S(1)}, f32[1536,1]{0,1:T(1,128)}, u32[]{:S(2)}) copy-start(f32[1536,1]{0,1:T(1,128)} %broadcast_in_dim.30) | copy-start | bytes 18436
  789.2 77.1 %copy-start.103 = (pred[256]{0:T(512)(128)(4,1)S(1)}, pred[256]{0:T(512)(128)(4,1)}, u32[]{:S(2)}) copy-start(pred[256]{0:T(512)(128)(4,1)} %copy-done.102) | copy-start | bytes 772
  922.5 81.8 %collective-permute-start.1 = (f32[1536,3]{0,1:T(4,128)S(1)}, f32[1536,3]{0,1:T(4,128)S(1)}, u32[]{:S(2)}, u32[]{:S(2)}) collective-permute-start(f32[1536,3]{0,1:T(4,128)S(1)} %slice.974), channel_id=1, source_target_pairs={{1,0},{2,1},{3,2},{4,3},{5,4},{6,5},{7,6},{9,8},{10,9},{11,10},{12... | collective-permute-start | bytes 55304 | tf_op jit(solution)/shard_map/ppermute | solution.py:23
  1098.4 1967.5 %all-reduce.70.cloned.1.call-start = ((), (), s32[]{:S(2)}) async-start(), calls=%async_computation.6 | async-start | bytes 14770176 | tf_op jit(solution)/shard_map/psum | solution.py:287
  (119 other events, 775.7 us)
Sparse Core Ops, SparseCore 0:
  10.2 63.1 all-gather.10
  75.6 59.0 all-gather.12
  136.9 59.3 all-gather.14
  198.2 98.5 all-gather.16
  298.7 98.1 all-gather.18
  398.9 98.4 all-gather.20
  1098.5 1748.0 all-reduce.71
  2928.9 136.9 all-reduce.69
where the time goes:
time: 3120 us; the launch traced here: 3100 us
  waiting for transfers between devices  2000 us (64%)
  local copies, waits for them, and re-layouts  688 us (22%)
  other arithmetic  153 us (5%)
  blocking collectives  126 us (4%)
  matrix products  113 us (4%)
    unnamed x9, waiting for transfers between devices  1750 us
    slice x57, local copies, waits for them, and re-layouts, reverse_local(): lax.associative_scan(affine, (factor, jnp.flip(grad_state, axis=1)), axis=1)  138 us
    psum x1, waiting for transfers between devices, body(): summed = lax.psum(shared.reshape(-1), 'rows')  129 us
    all_gather x4, blocking collectives, prefix(): pieces = jax.tree.map(lambda part: lax.all_gather(part, axis), value)  126 us
    slice x52, local copies, waits for them, and re-layouts, body(): lax.associative_scan(affine, (decay_rate, lru_input), axis=1)  98.4 us
    reshape x1, local copies, waits for them, and re-layouts, body(): summed = lax.psum(shared.reshape(-1), 'rows')  82.1 us
    unnamed x291, local copies, waits for them, and re-layouts  79.2 us
    reshape x15, local copies, waits for them, and re-layouts, flatten_rows(): source.reshape(row_count, -1)  62.4 us
  transfers between devices with their start and end apart: 10, of which 5 were waited for; matrix products, arithmetic and copies ran while one was open for 14% of the time, Pallas kernels for 0%

commit v1 on v0

--- a/solution.py
+++ b/solution.py
@@ -4,6 +4,8 @@
 import jax
 import jax.numpy as jnp
 from jax import lax
+from jax.experimental import pallas as pl
+from jax.experimental.pallas import tpu as pltpu
 from jax.sharding import PartitionSpec as P
 
 D = 1024
@@ -339,6 +341,1237 @@
     )
 
 
+MESH = pl.DeviceIdType.MESH
+LOW = jnp.bfloat16
+F32 = jnp.float32
+VMEM_BYTES = 60 * 2**20
+TILE = 8
+GELU_A = math.sqrt(2.0 / math.pi)
+GELU_B = 0.044715
+
+
+def nt(left, right):
+    return lax.dot_general(left, right, (((1,), (1,)), ((), ())), preferred_element_type=F32)
+
+
+def nn(left, right):
+    return lax.dot_general(left, right, (((1,), (0,)), ((), ())), preferred_element_type=F32)
+
+
+def tn(left, right):
+    return lax.dot_general(left, right, (((0,), (0,)), ((), ())), preferred_element_type=F32)
+
+
+def gelu_pair(values):
+    squared = values * values
+    bend = jnp.tanh(GELU_A * values * (1.0 + GELU_B * squared))
+    half = 0.5 * (1.0 + bend)
+    slope = half + 0.5 * values * (1.0 - bend * bend) * GELU_A * (1.0 + 3.0 * GELU_B * squared)
+    return values * half, slope
+
+
+class Spot:
+    def __init__(self):
+        self.r = lax.axis_index("rows")
+        self.c = lax.axis_index("chan")
+        self.z = lax.div(self.c, 2)
+        self.y = lax.rem(self.c, 2)
+        self.r_core = self.r + 1 - 2 * lax.rem(self.r, 2)
+        self.r_x = lax.rem(self.r + 2, 4)
+        self.core = (self.r_core, self.c)
+        self.x = (self.r_x, self.c)
+        self.c_y = self.c + 1 - 2 * self.y
+        self.ymate = (self.r, self.c_y)
+        self.up = (self.r, lax.rem(self.c + 2, 8))
+        self.dn = (self.r, lax.rem(self.c + 6, 8))
+
+
+def greet(always, maybe=()):
+    barrier = pltpu.get_barrier_semaphore()
+    count = len(always)
+    for device in always:
+        pl.semaphore_signal(barrier, inc=1, device_id=device, device_id_type=MESH)
+    for device, there in maybe:
+
+        @pl.when(there)
+        def _(device=device):
+            pl.semaphore_signal(barrier, inc=1, device_id=device, device_id_type=MESH)
+
+        count = count + jnp.where(there, 1, 0)
+    pl.semaphore_wait(barrier, count)
+
+
+def push(source, target, sems, index, device):
+    return pltpu.make_async_remote_copy(
+        src_ref=source,
+        dst_ref=target,
+        send_sem=sems[0].at[index],
+        recv_sem=sems[1].at[index],
+        device_id=device,
+        device_id_type=MESH,
+    )
+
+
+def landed(me, target, sems, index):
+    push(target, target, sems, index, me.ymate).wait_recv()
+
+
+def sem_pair(count):
+    return [pltpu.SemaphoreType.DMA((count,)), pltpu.SemaphoreType.DMA((count,))]
+
+
+def comm_params(collective_id):
+    return pltpu.CompilerParams(
+        collective_id=collective_id, has_side_effects=True, vmem_limit_bytes=VMEM_BYTES
+    )
+
+
+def plain_params():
+    return pltpu.CompilerParams(
+        dimension_semantics=("arbitrary",), vmem_limit_bytes=VMEM_BYTES
+    )
+
+
+ANYWHERE = pl.BlockSpec(memory_space=pl.ANY)
+IN_VMEM = pl.BlockSpec(memory_space=pltpu.VMEM)
+
+
+def gather_kernel(
+    wm, nrm, cot, starts, wq, nall, call, halo, starts_all,
+    loc, xs, xr, cs, cr, hs, hr, ss, sr, ys, yr, us, ds, zr,
+):
+    me = Spot()
+    r, c, z, y = me.r, me.c, me.z, me.y
+    rows = wm.shape[1]
+    piece = 48
+    per = rows // piece
+    greet(
+        [me.core, me.x, (me.r_x + 1 - 2 * lax.rem(me.r_x, 2), c), me.ymate],
+        [(me.up, z < 3), (me.dn, z > 0)]
+        + [((row, lax.rem(c + 1, 8)), c < 7) for row in range(4)]
+        + [((row, lax.rem(c + 7, 8)), c > 0) for row in range(4)],
+    )
+    tail = nrm.shape[0] - halo.shape[1]
+    own = pltpu.make_async_copy(wm, wq.at[:, pl.ds(y * rows, rows)], loc.at[0])
+
+    @pl.when(z == r)
+    def _():
+        own.start()
+
+    x_n = push(nrm, nall.at[r], (xs, xr), 0, me.x)
+    x_n.start()
+    c_n = push(nrm, nall.at[r], (cs, cr), 0, me.core)
+    c_n.start()
+    diag = (me.r_x + 1 - 2 * lax.rem(me.r_x, 2), c)
+    s_copies = [
+        push(starts, starts_all.at[r], (ss, sr), i, device)
+        for i, device in enumerate((me.core, me.x, diag))
+    ]
+    for copy in s_copies:
+        copy.start()
+    halo_copies = [
+        push(nrm.at[pl.ds(tail, halo.shape[1])], halo.at[r], (hs, hr), i, (lax.rem(r + i, 4), lax.rem(c + 1, 8)))
+        for i in range(4)
+    ]
+
+    @pl.when(c < 7)
+    def _():
+        for copy in halo_copies:
+            copy.start()
+
+    here_n = pltpu.make_async_copy(nrm, nall.at[r], loc.at[1])
+    here_n.start()
+    here_c = pltpu.make_async_copy(cot, call.at[r], loc.at[2])
+    here_c.start()
+    here_s = pltpu.make_async_copy(starts, starts_all.at[r], loc.at[3])
+    here_s.start()
+    halo_fill = [
+        pltpu.make_async_copy(nrm.at[pl.ds(tail, halo.shape[1])], halo.at[i], loc.at[4 + i])
+        for i in range(4)
+    ]
+
+    @pl.when(c == 0)
+    def _():
+        for copy in halo_fill:
+            copy.start()
+
+    c_c = push(cot, call.at[r], (cs, cr), 1, me.core)
+    c_c.start()
+    x_c = push(cot, call.at[r], (xs, xr), 1, me.x)
+    fwd_n = push(nall.at[me.r_x], nall.at[me.r_x], (cs, cr), 2, me.core)
+    fwd_c = push(call.at[me.r_x], call.at[me.r_x], (cs, cr), 3, me.core)
+
+    @pl.when(z == r)
+    def _():
+        own.wait()
+
+    count = 3 * per
+    go_up = jnp.logical_and(z >= r, z < 3)
+    go_dn = jnp.logical_and(z <= r, z > 0)
+
+    def slab(k, half):
+        return wq.at[k // per, pl.ds(half * rows + (k % per) * piece, piece)]
+
+    y_copies = [push(slab(k, y), slab(k, y), (ys, yr), k, me.ymate) for k in range(count)]
+    up_copies = [push(slab(k, y), slab(k, y), (us, zr), k, me.up) for k in range(count)]
+    dn_copies = [push(slab(k, y), slab(k, y), (ds, zr), k, me.dn) for k in range(count)]
+
+    def sent(k):
+        y_copies[k].wait_send()
+
+        @pl.when(go_up)
+        def _():
+            up_copies[k].wait_send()
+
+        @pl.when(go_dn)
+        def _():
+            dn_copies[k].wait_send()
+
+    for k in range(count):
+
+        @pl.when(z != r)
+        def _(k=k):
+            landed(me, slab(k, y), (us, zr), k)
+
+        y_copies[k].start()
+
+        @pl.when(go_up)
+        def _(k=k):
+            up_copies[k].start()
+
+        @pl.when(go_dn)
+        def _(k=k):
+            dn_copies[k].start()
+
+        if k == per:
+            x_c.start()
+        if k == 2 * per:
+            x_n.wait_recv()
+            fwd_n.start()
+        if k >= 3:
+            sent(k - 3)
+    for k in range(count - 3, count):
+        sent(k)
+    x_c.wait_recv()
+    fwd_c.start()
+    for k in range(count):
+        y_copies[k].wait_recv()
+    x_n.wait_send()
+    x_c.wait_send()
+    for copy in [c_n, c_c, fwd_n, fwd_c]:
+        copy.wait_send()
+        copy.wait_recv()
+    for copy in s_copies:
+        copy.wait_send()
+        copy.wait_recv()
+
+    @pl.when(c < 7)
+    def _():
+        for copy in halo_copies:
+            copy.wait_send()
+
+    @pl.when(c > 0)
+    def _():
+        for i in range(4):
+            landed(me, halo.at[i], (hs, hr), i)
+
+    @pl.when(c == 0)
+    def _():
+        for copy in halo_fill:
+            copy.wait()
+
+    here_n.wait()
+    here_c.wait()
+    here_s.wait()
+
+
+def gather(wm, nrm, cot, starts):
+    rows = wm.shape[1]
+    count = 3 * rows // 48
+    sd = jax.ShapeDtypeStruct
+    return pl.pallas_call(
+        gather_kernel,
+        name="gather_front",
+        out_shape=[
+            sd((3, 2 * rows, D), LOW),
+            sd((4,) + nrm.shape, LOW),
+            sd((4,) + cot.shape, LOW),
+            sd((4, 16, D), LOW),
+            sd((4,) + starts.shape, starts.dtype),
+        ],
+        in_specs=[ANYWHERE] * 4,
+        out_specs=[ANYWHERE] * 5,
+        scratch_shapes=[pltpu.SemaphoreType.DMA((8,))]
+        + sem_pair(2) + sem_pair(4) + sem_pair(4) + sem_pair(3) + sem_pair(count)
+        + [pltpu.SemaphoreType.DMA((count,))] * 3,
+        compiler_params=comm_params(1),
+    )(wm, nrm, cot, starts)
+
+
+def decay_terms(rec, softplus_row, reset):
+    log_decay = -8.0 * rec * softplus_row
+    decay = jnp.exp(log_decay)
+    twice = 2.0 * log_decay
+    series = twice * (
+        1.0
+        + twice * (1 / 2 + twice * (1 / 6 + twice * (1 / 24 + twice * (1 / 120 + twice * (1 / 720)))))
+    )
+    gap = jnp.where(twice > -0.25, -series, 1.0 - jnp.exp(twice))
+    return decay, jnp.where(reset, 1.0, jnp.sqrt(gap))
+
+
+def mixer_one_kernel(
+    nrm, halo, wg, wl, vec, taps, rgate, igate, mask,
+    gate_pre, lext, conv_o, rec_o, open_o, a_o, b_o, tot,
+):
+    length = nrm.shape[1]
+    wide = wg.shape[1]
+    tokens = nrm[0]
+    gate_pre[0] = nt(tokens, wg[0]) + vec[0:1]
+    lifted = nt(tokens, wl[0]) + vec[1:2]
+    lext[0, 0:8] = (nt(halo[0], wl[0]) + vec[1:2])[8:16]
+    lext[0, pl.ds(8, length)] = lifted
+    conv = vec[2:3] + taps[0:1] * lifted
+    for k in range(1, 4):
+        conv = conv + taps[k : k + 1] * lext[0, pl.ds(8 - k, length)] * mask[0, :, k - 1 : k]
+    conv_o[0] = conv
+    conv_low = conv.astype(LOW)
+    rec = jax.nn.sigmoid(nn(conv_low, rgate[...]) + vec[3:4])
+    opening = jax.nn.sigmoid(nn(conv_low, igate[...]) + vec[4:5])
+    rec_o[0] = rec
+    open_o[0] = opening
+    reset = mask[0, :, 3:4] > 0.5
+    decay, scaling = decay_terms(rec, vec[5:6], reset)
+    decay = jnp.where(reset, 0.0, decay)
+    a = decay.reshape(length // TILE, TILE, wide)
+    b = (scaling * opening * conv).reshape(length // TILE, TILE, wide)
+    row = lax.broadcasted_iota(jnp.int32, a.shape, 1)
+    for step in (1, 2, 4):
+        earlier = row >= step
+        b = b + a * jnp.where(earlier, pltpu.roll(b, step, 1), 0.0)
+        a = a * jnp.where(earlier, pltpu.roll(a, step, 1), 1.0)
+    a_o[0] = a.reshape(length, wide)
+    b_o[0] = b.reshape(length, wide)
+    product = jnp.ones((1, wide), F32)
+    state = jnp.zeros((1, wide), F32)
+    for t in range(length // TILE):
+        last = t * TILE + TILE - 1
+        a_last = a_o[0, last : last + 1]
+        state = b_o[0, last : last + 1] + a_last * state
+        product = product * a_last
+    tot[0, 0:1] = product
+    tot[0, 1:2] = state
+
+
+def whole(shape):
+    return pl.BlockSpec(shape, lambda s: (0,) * len(shape))
+
+
+def per_seq(shape):
+    return pl.BlockSpec((1,) + shape, lambda s: (s,) + (0,) * len(shape))
+
+
+def mixer_one(nall, halo, wq, vec, taps, rgate, igate, mask):
+    seqs, length, width = nall.shape
+    wide = wq.shape[1]
+    sd = jax.ShapeDtypeStruct
+    full = sd((seqs, length, wide), F32)
+    return pl.pallas_call(
+        mixer_one_kernel,
+        name="mixer_forward_gates",
+        grid=(seqs,),
+        in_specs=[
+            per_seq((length, width)),
+            per_seq((16, width)),
+            pl.BlockSpec((1, wide, width), lambda s: (0, 0, 0)),
+            pl.BlockSpec((1, wide, width), lambda s: (1, 0, 0)),
+            whole(vec.shape),
+            whole(taps.shape),
+            whole(rgate.shape),
+            whole(igate.shape),
+            per_seq((length, 8)),
+        ],
+        out_specs=[per_seq((length, wide)), per_seq((length + 8, wide))]
+        + [per_seq((length, wide))] * 5
+        + [per_seq((2, wide))],
+        out_shape=[full, sd((seqs, length + 8, wide), F32), full, full, full, full, full,
+                   sd((seqs, 2, wide), F32)],
+        compiler_params=plain_params(),
+    )(nall, halo, wq, wq, vec, taps, rgate, igate, mask)
+
+
+def prefix_kernel(backward, totals, start, slots, send, recv):
+    me = Spot()
+    r, c = me.r, me.c
+    sign = -1 if backward else 1
+    steps = c if backward else 7 - c
+    behind = (7 - c) if backward else c
+    greet(
+        [],
+        [((r, lax.rem(c + 8 + sign * d, 8)), d <= steps) for d in range(1, 8)]
+        + [((r, lax.rem(c + 8 - sign * d, 8)), d <= behind) for d in range(1, 8)],
+    )
+    copies = [
+        push(totals, slots.at[d], (send, recv), d, (r, lax.rem(c + 8 + sign * d, 8))) for d in range(1, 8)
+    ]
+    for d in range(1, 8):
+
+        @pl.when(d <= steps)
+        def _(d=d):
+            copies[d - 1].start()
+
+    start[...] = jnp.zeros_like(start)
+    for d in range(7, 0, -1):
+
+        @pl.when(d <= behind)
+        def _(d=d):
+            landed(me, slots.at[d], (send, recv), d)
+            start[...] = slots[d, :, 0] * start[...] + slots[d, :, 1]
+
+    for d in range(1, 8):
+
+        @pl.when(d <= steps)
+        def _(d=d):
+            copies[d - 1].wait_send()
+
+
+def carry_in(totals, backward):
+    seqs, _, wide = totals.shape
+    return pl.pallas_call(
+        partial(prefix_kernel, backward),
+        name="carry_back" if backward else "carry_on",
+        out_shape=jax.ShapeDtypeStruct((seqs, wide), F32),
+        in_specs=[IN_VMEM],
+        out_specs=IN_VMEM,
+        scratch_shapes=[pltpu.VMEM((8,) + totals.shape, F32)] + sem_pair(8),
+        compiler_params=comm_params(3 if backward else 2),
+    )(totals)
+
+
+def mixer_two_kernel(a, b, start, gate_pre, wo, state_o, mixed_o, part):
+    tiles = a.shape[1] // TILE
+    state = start[0]
+    for t in range(tiles):
+        rows = pl.ds(t * TILE, TILE)
+        now = b[0, rows] + a[0, rows] * state
+        state_o[0, rows] = now
+        state = now[TILE - 1 : TILE]
+    gate_val, _ = gelu_pair(gate_pre[0])
+    mixed = (state_o[0] * gate_val).astype(LOW)
+    mixed_o[0] = mixed
+    part[0] = nn(mixed, wo[0]).astype(LOW)
+
+
+def mixer_two(a, b, start, gate_pre, wq):
+    seqs, length, wide = a.shape
+    width = wq.shape[2]
+    sd = jax.ShapeDtypeStruct
+    block = per_seq((length, wide))
+    return pl.pallas_call(
+        mixer_two_kernel,
+        name="mixer_forward_state",
+        grid=(seqs,),
+        in_specs=[block, block, per_seq((1, wide)), block,
+                  pl.BlockSpec((1, wide, width), lambda s: (2, 0, 0))],
+        out_specs=[block, block, per_seq((length, width))],
+        out_shape=[sd(a.shape, F32), sd(a.shape, LOW), sd((seqs, length, width), LOW)],
+        compiler_params=plain_params(),
+    )(a, b, start.reshape(seqs, 1, wide), gate_pre, wq)
+
+
+RS_CHUNKS = 4
+
+
+def rows_sum_start(me, part, mate, sems):
+    length = part.shape[1]
+    step = length // RS_CHUNKS
+    far = lax.rem(me.r_core + 2, 4)
+    copies = []
+    for block, owner in enumerate((far, me.r_core)):
+        for k in range(RS_CHUNKS):
+            rows = pl.ds(k * step, step)
+            copies.append(
+                push(part.at[owner, rows], mate.at[block, rows], sems, block * RS_CHUNKS + k, me.core)
+            )
+    for copy in copies:
+        copy.start()
+    return copies
+
+
+def rows_sum_cross(me, part, mate, out_x, in_x, copies, sems):
+    length = part.shape[1]
+    step = length // RS_CHUNKS
+    crossing = []
+    for k in range(RS_CHUNKS):
+        rows = pl.ds(k * step, step)
+        copies[k].wait_recv()
+        out_x[rows] = (part[me.r_x, rows].astype(F32) + mate[0, rows].astype(F32)).astype(LOW)
+        copy = push(out_x.at[rows], in_x.at[rows], sems, k, me.x)
+        copy.start()
+        crossing.append(copy)
+    return crossing
+
+
+def rows_sum_chunk(me, part, mate, in_x, copies, crossing, k):
+    length = part.shape[1]
+    step = length // RS_CHUNKS
+    rows = pl.ds(k * step, step)
+    copies[RS_CHUNKS + k].wait_recv()
+    crossing[k].wait_recv()
+    return part[me.r, rows].astype(F32) + mate[1, rows].astype(F32) + in_x[rows].astype(F32)
+
+
+def finish_sends(copies):
+    for copy in copies:
+        copy.wait_send()
+
+
+def rows_sum_scratch(length, width):
+    return [
+        pltpu.VMEM((2, length, width), LOW),
+        pltpu.VMEM((length, width), LOW),
+        pltpu.VMEM((length, width), LOW),
+    ] + sem_pair(2 * RS_CHUNKS) + sem_pair(RS_CHUNKS)
+
+
+def spread_chunk(me, all_ref, k, sems_x, sems_c):
+    length = all_ref.shape[1]
+    step = length // RS_CHUNKS
+    rows = pl.ds(k * step, step)
+    mine = all_ref.at[me.r, rows]
+    copies = [
+        push(mine, mine, sems_x, k, me.x),
+        push(mine, mine, sems_c, k, me.core),
+    ]
+    for copy in copies:
+        copy.start()
+    return copies
+
+
+def spread_rest(me, all_ref, first, sems_c):
+    length = all_ref.shape[1]
+    step = length // RS_CHUNKS
+    passed = []
+    for k in range(RS_CHUNKS):
+        first[k][0].wait_recv()
+        theirs = all_ref.at[me.r_x, pl.ds(k * step, step)]
+        copy = push(theirs, theirs, sems_c, RS_CHUNKS + k, me.core)
+        copy.start()
+        passed.append(copy)
+    for k in range(RS_CHUNKS):
+        first[k][0].wait_send()
+        first[k][1].wait()
+        passed[k].wait()
+
+
+def resid_kernel(
+    part, inputs, bias, gain, resid, nall,
+    mate, out_x, in_x, ms, mr, xs, xr, ax, bx, ac, bc,
+):
+    me = Spot()
+    greet([me.core, me.x])
+    step = inputs.shape[0] // RS_CHUNKS
+    copies = rows_sum_start(me, part, mate, (ms, mr))
+    crossing = rows_sum_cross(me, part, mate, out_x, in_x, copies, (xs, xr))
+    first = []
+    for k in range(RS_CHUNKS):
+        rows = pl.ds(k * step, step)
+        total = rows_sum_chunk(me, part, mate, in_x, copies, crossing, k)
+        res = inputs[rows].astype(F32) + total + bias[...]
+        resid[rows] = res
+        scale = lax.rsqrt(jnp.mean(res * res, axis=-1, keepdims=True) + EPSILON)
+        nall[me.r, rows] = (res * scale * gain[...]).astype(LOW)
+        first.append(spread_chunk(me, nall, k, (ax, bx), (ac, bc)))
+    spread_rest(me, nall, first, (ac, bc))
+    finish_sends(copies + crossing)
+
+
+def resid_step(part, inputs, bias, gain):
+    sd = jax.ShapeDtypeStruct
+    length, width = inputs.shape
+    return pl.pallas_call(
+        resid_kernel,
+        name="resid_sum",
+        out_shape=[sd(inputs.shape, F32), sd(part.shape, LOW)],
+        in_specs=[IN_VMEM] * 4,
+        out_specs=[IN_VMEM] * 2,
+        scratch_shapes=rows_sum_scratch(length, width)
+        + sem_pair(RS_CHUNKS) + sem_pair(2 * RS_CHUNKS),
+        compiler_params=comm_params(4),
+    )(part, inputs, bias, gain)
+
+
+def grad_resid_kernel(
+    part, cot, resid, gain, gresid, ball, gains,
+    mate, out_x, in_x, ms, mr, xs, xr, ax, bx, ac, bc,
+):
+    me = Spot()
+    greet([me.core, me.x])
+    step = cot.shape[0] // RS_CHUNKS
+    copies = rows_sum_start(me, part, mate, (ms, mr))
+    crossing = rows_sum_cross(me, part, mate, out_x, in_x, copies, (xs, xr))
+    first = []
+    gain_sum = 0.0
+    bias_sum = 0.0
+    for k in range(RS_CHUNKS):
+        rows = pl.ds(k * step, step)
+        grad = rows_sum_chunk(me, part, mate, in_x, copies, crossing, k)
+        res = resid[rows]
+        scale = lax.rsqrt(jnp.mean(res * res, axis=-1, keepdims=True) + EPSILON)
+        gain_sum = gain_sum + jnp.sum(grad * res * scale, axis=0, keepdims=True)
+        pulled = grad * gain[...]
+        inner = jnp.mean(pulled * res, axis=-1, keepdims=True)
+        total = cot[rows].astype(F32) + scale * pulled - res * (scale * scale * scale * inner)
+        bias_sum = bias_sum + jnp.sum(total, axis=0, keepdims=True)
+        gresid[rows] = total
+        ball[me.r, rows] = total.astype(LOW)
+        first.append(spread_chunk(me, ball, k, (ax, bx), (ac, bc)))
+    gains[0:1] = gain_sum
+    gains[1:2] = bias_sum
+    spread_rest(me, ball, first, (ac, bc))
+    finish_sends(copies + crossing)
+
+
+def grad_resid_step(part, cot, resid, gain):
+    sd = jax.ShapeDtypeStruct
+    length, width = cot.shape
+    return pl.pallas_call(
+        grad_resid_kernel,
+        name="grad_resid_sum",
+        out_shape=[sd(cot.shape, F32), sd(part.shape, LOW), sd((2, width), F32)],
+        in_specs=[IN_VMEM] * 4,
+        out_specs=[IN_VMEM] * 3,
+        scratch_shapes=rows_sum_scratch(length, width)
+        + sem_pair(RS_CHUNKS) + sem_pair(2 * RS_CHUNKS),
+        compiler_params=comm_params(5),
+    )(part, cot, resid, gain)
+
+
+def mlp_kernel(
+    nall, call, wg, wu, wd, part, gpart, dg_o, du_o, dd_o,
+    acc_out, acc_in, acc_g, acc_u, acc_d,
+):
+    block = pl.program_id(0)
+    length = nall.shape[1]
+
+    @pl.when(block == 0)
+    def _():
+        acc_out[...] = jnp.zeros_like(acc_out)
+        acc_in[...] = jnp.zeros_like(acc_in)
+
+    acc_g[...] = jnp.zeros_like(acc_g)
+    acc_u[...] = jnp.zeros_like(acc_u)
+    acc_d[...] = jnp.zeros_like(acc_d)
+
+    @pl.loop(0, nall.shape[0])
+    def _(s):
+        tokens = nall[s]
+        cot = call[s]
+        gate = nt(tokens, wg[...])
+        up = nt(tokens, wu[...])
+        grad_hidden = nt(cot, wd[...])
+        gate_val, slope = gelu_pair(gate)
+        hidden = (gate_val * up).astype(LOW)
+        grad_gate = (grad_hidden * up * slope).astype(LOW)
+        grad_up = (grad_hidden * gate_val).astype(LOW)
+        acc_out[s] += nn(hidden, wd[...])
+        acc_in[s] += nn(grad_gate, wg[...]) + nn(grad_up, wu[...])
+        acc_d[...] += tn(hidden, cot)
+        acc_g[...] += tn(grad_gate, tokens)
+        acc_u[...] += tn(grad_up, tokens)
+
+    dg_o[...] = acc_g[...].astype(LOW)
+    du_o[...] = acc_u[...].astype(LOW)
+    dd_o[...] = acc_d[...].astype(LOW)
+
+    @pl.when(block == pl.num_programs(0) - 1)
+    def _():
+        part[...] = acc_out[...].astype(LOW)
+        gpart[...] = acc_in[...].astype(LOW)
+
+
+def mlp(nall, call, wg, wu, wd):
+    hidden, width = wg.shape
+    blocks = 2
+    cut = hidden // blocks
+    sd = jax.ShapeDtypeStruct
+    weight = pl.BlockSpec((cut, width), lambda h: (h, 0))
+    return pl.pallas_call(
+        mlp_kernel,
+        name="mlp_both_ways",
+        grid=(blocks,),
+        in_specs=[whole(nall.shape), whole(call.shape), weight, weight, weight],
+        out_specs=[whole(nall.shape), whole(nall.shape), weight, weight, weight],
+        out_shape=[sd(nall.shape, LOW)] * 2 + [sd(wg.shape, LOW)] * 3,
+        scratch_shapes=[pltpu.VMEM(nall.shape, F32)] * 2 + [pltpu.VMEM((cut, width), F32)] * 3,
+        compiler_params=plain_params(),
+    )(nall, call, wg, wu, wd)
+
+
+def mixer_three_kernel(
+    ball, wo, gate_pre, state, mixed, rec, vec, mask,
+    gate_low, gs_o, a_o, b_o, tot, dwo, sums, acc_w, acc_b,
+):
+    seq = pl.program_id(0)
+    length, wide = rec.shape[1], rec.shape[2]
+
+    @pl.when(seq == 0)
+    def _():
+        acc_w[...] = jnp.zeros_like(acc_w)
+        acc_b[...] = jnp.zeros_like(acc_b)
+
+    branch = ball[0]
+    grad_mixed = nt(branch, wo[0])
+    gate_val, slope = gelu_pair(gate_pre[0])
+    grad_gate = grad_mixed * state[0] * slope
+    gate_low[0] = grad_gate.astype(LOW)
+    acc_b[...] += jnp.sum(grad_gate, axis=0, keepdims=True)
+    acc_w[...] += tn(mixed[0], branch)
+    grad_state = grad_mixed * gate_val
+    gs_o[0] = grad_state
+    reset = mask[0, :, 3:4] > 0.5
+    decay = jnp.where(reset, 0.0, jnp.exp(-8.0 * rec[0] * vec[5:6]))
+    a = decay.reshape(length // TILE, TILE, wide)
+    b = (decay * grad_state).reshape(length // TILE, TILE, wide)
+    row = lax.broadcasted_iota(jnp.int32, a.shape, 1)
+    for step in (1, 2, 4):
+        later = row < TILE - step
+        b = b + a * jnp.where(later, pltpu.roll(b, TILE - step, 1), 0.0)
+        a = a * jnp.where(later, pltpu.roll(a, TILE - step, 1), 1.0)
+    a_o[0] = a.reshape(length, wide)
+    b_o[0] = b.reshape(length, wide)
+    product = jnp.ones((1, wide), F32)
+    carry = jnp.zeros((1, wide), F32)
+    for t in range(length // TILE - 1, -1, -1):
+        head = t * TILE
+        a_head = a_o[0, head : head + 1]
+        carry = b_o[0, head : head + 1] + a_head * carry
+        product = product * a_head
+    tot[0, 0:1] = product
+    tot[0, 1:2] = carry
+
+    @pl.when(seq == pl.num_programs(0) - 1)
+    def _():
+        dwo[...] = acc_w[...].astype(LOW)
+        sums[...] = acc_b[...]
+
+
+def mixer_three(ball, wq, gate_pre, state, mixed, rec, vec, mask):
+    seqs, length, wide = rec.shape
+    width = wq.shape[2]
+    sd = jax.ShapeDtypeStruct
+    block = per_seq((length, wide))
+    full = sd(rec.shape, F32)
+    return pl.pallas_call(
+        mixer_three_kernel,
+        name="mixer_backward_state",
+        grid=(seqs,),
+        in_specs=[per_seq((length, width)),
+                  pl.BlockSpec((1, wide, width), lambda s: (2, 0, 0)),
+                  block, block, block, block, whole(vec.shape), per_seq((length, 8))],
+        out_specs=[block, block, block, block, per_seq((2, wide)),
+                   whole((wide, width)), whole((1, wide))],
+        out_shape=[sd(rec.shape, LOW), full, full, full, sd((seqs, 2, wide), F32),
+                   sd((wide, width), LOW), sd((1, wide), F32)],
+        scratch_shapes=[pltpu.VMEM((wide, width), F32), pltpu.VMEM((1, wide), F32)],
+        compiler_params=plain_params(),
+    )(ball, wq, gate_pre, state, mixed, rec, vec, mask)
+
+
+def mixer_four_kernel(
+    a, b, gs, carry_in_ref, state, start, conv_r, rec_r, open_r, vec, rgate, igate, mask,
+    grad_conv, drg, dig, sums, ext, prev_ext, acc_s,
+):
+    seq = pl.program_id(0)
+    length, wide = rec_r.shape[1], rec_r.shape[2]
+
+    @pl.when(seq == 0)
+    def _():
+        drg[...] = jnp.zeros_like(drg)
+        dig[...] = jnp.zeros_like(dig)
+        acc_s[...] = jnp.zeros_like(acc_s)
+
+    carry = carry_in_ref[0]
+    ext[pl.ds(length, TILE)] = jnp.broadcast_to(carry, (TILE, wide))
+    for t in range(length // TILE - 1, -1, -1):
+        rows = pl.ds(t * TILE, TILE)
+        now = b[0, rows] + a[0, rows] * carry
+        ext[rows] = now
+        carry = now[0:1]
+    carried = gs[0] + ext[pl.ds(1, length)]
+    prev_ext[0:TILE] = jnp.broadcast_to(start[0], (TILE, wide))
+    prev_ext[pl.ds(TILE, length)] = state[0]
+    previous = prev_ext[pl.ds(TILE - 1, length)]
+    rec, opening, conv = rec_r[0], open_r[0], conv_r[0]
+    reset = mask[0, :, 3:4] > 0.5
+    decay, scaling = decay_terms(rec, vec[5:6], reset)
+    pulled = carried * scaling
+    grad_opening = pulled * conv
+    direct = pulled * opening
+    grad_log = carried * (previous * decay - opening * conv * (decay * decay / scaling))
+    grad_log = jnp.where(reset, 0.0, grad_log)
+    grad_rec = grad_log * (-8.0 * vec[5:6])
+    grad_rpre = grad_rec * rec * (1.0 - rec)
+    grad_opre = grad_opening * opening * (1.0 - opening)
+    r_low, o_low, conv_low = grad_rpre.astype(LOW), grad_opre.astype(LOW), conv.astype(LOW)
+    total = direct + nt(r_low, rgate[...]) + nt(o_low, igate[...])
+    grad_conv[0] = total
+    drg[...] += tn(conv_low, r_low)
+    dig[...] += tn(conv_low, o_low)
+    acc_s[0:1] += jnp.sum(grad_rpre, axis=0, keepdims=True)
+    acc_s[1:2] += jnp.sum(grad_opre, axis=0, keepdims=True)
+    acc_s[2:3] += jnp.sum(grad_log * rec, axis=0, keepdims=True) * (8.0 * vec[6:7])
+    acc_s[3:4] += jnp.sum(total, axis=0, keepdims=True)
+    sums[...] = acc_s[...]
+
+
+def mixer_four(a, b, gs, carry, state, start, conv, rec, opening, vec, rgate, igate, mask):
+    seqs, length, wide = rec.shape
+    sd = jax.ShapeDtypeStruct
+    block = per_seq((length, wide))
+    one = per_seq((1, wide))
+    square = whole((wide, wide))
+    return pl.pallas_call(
+        mixer_four_kernel,
+        name="mixer_backward_gates",
+        grid=(seqs,),
+        in_specs=[block, block, block, one, block, one, block, block, block,
+                  whole(vec.shape), square, square, per_seq((length, 8))],
+        out_specs=[block, square, square, whole((4, wide))],
+        out_shape=[sd(rec.shape, F32), sd((wide, wide), F32), sd((wide, wide), F32),
+                   sd((4, wide), F32)],
+        scratch_shapes=[pltpu.VMEM((length + TILE, wide), F32)] * 2 + [pltpu.VMEM((4, wide), F32)],
+        compiler_params=plain_params(),
+    )(a, b, gs, carry.reshape(seqs, 1, wide), state, start.reshape(seqs, 1, wide), conv, rec,
+      opening, vec, rgate, igate, mask)
+
+
+def mixer_five_kernel(
+    grad_conv, head, lext, taps, mask, gate_low, nrm, wg, wl,
+    part, dwg, dwl, sums, ext, acc_g, acc_l, acc_s,
+):
+    seq = pl.program_id(0)
+    length, wide = grad_conv.shape[1], grad_conv.shape[2]
+
+    @pl.when(seq == 0)
+    def _():
+        acc_g[...] = jnp.zeros_like(acc_g)
+        acc_l[...] = jnp.zeros_like(acc_l)
+        acc_s[...] = jnp.zeros_like(acc_s)
+
+    grad = grad_conv[0]
+    ext[pl.ds(0, length)] = grad
+    ext[pl.ds(length, TILE)] = head[0]
+    grad_lifted = taps[0:1] * grad
+    acc_s[0:1] += jnp.sum(grad * lext[0, pl.ds(TILE, length)], axis=0, keepdims=True)
+    for k in range(1, 4):
+        grad_lifted = grad_lifted + taps[k : k + 1] * ext[pl.ds(k, length)] * mask[0, :, 3 + k : 4 + k]
+        behind = lext[0, pl.ds(TILE - k, length)] * mask[0, :, k - 1 : k]
+        acc_s[k : k + 1] += jnp.sum(grad * behind, axis=0, keepdims=True)
+    acc_s[4:5] += jnp.sum(grad_lifted, axis=0, keepdims=True)
+    lift_low = grad_lifted.astype(LOW)
+    tokens = nrm[0]
+    part[0] = (nn(gate_low[0], wg[0]) + nn(lift_low, wl[0])).astype(LOW)
+    acc_g[...] += tn(gate_low[0], tokens)
+    acc_l[...] += tn(lift_low, tokens)
+
+    @pl.when(seq == pl.num_programs(0) - 1)
+    def _():
+        dwg[...] = acc_g[...].astype(LOW)
+        dwl[...] = acc_l[...].astype(LOW)
+        sums[...] = acc_s[...]
+
+
+def mixer_five(grad_conv, head, lext, taps, mask, gate_low, nall, wq):
+    seqs, length, wide = grad_conv.shape
+    width = wq.shape[2]
+    sd = jax.ShapeDtypeStruct
+    block = per_seq((length, wide))
+    return pl.pallas_call(
+        mixer_five_kernel,
+        name="mixer_backward_conv",
+        grid=(seqs,),
+        in_specs=[block, per_seq((TILE, wide)), per_seq((length + TILE, wide)), whole(taps.shape),
+                  per_seq((length, 8)), block, per_seq((length, width)),
+                  pl.BlockSpec((1, wide, width), lambda s: (0, 0, 0)),
+                  pl.BlockSpec((1, wide, width), lambda s: (1, 0, 0))],
+        out_specs=[per_seq((length, width)), whole((wide, width)), whole((wide, width)),
+                   whole((8, wide))],
+        out_shape=[sd((seqs, length, width), LOW), sd((wide, width), LOW), sd((wide, width), LOW),
+                   sd((8, wide), F32)],
+        scratch_shapes=[pltpu.VMEM((length + TILE, wide), F32), pltpu.VMEM((wide, width), F32),
+                        pltpu.VMEM((wide, width), F32), pltpu.VMEM((8, wide), F32)],
+        compiler_params=plain_params(),
+    )(grad_conv, head, lext, taps, mask, gate_low, nall, wq, wq)
+
+
+ORDER = (3, 0, 2, 1)
+
+
+def final_kernel(
+    gpart, opart, inputs, resid, gresid, gain, gains, even, odd,
+    output, ginputs, even_all, odd_own, gains_all,
+    g_mate, g_out, g_in, gs1, gr1, gs2, gr2,
+    o_mate, o_out, o_in, os1, or1, os2, or2,
+    y_even, z_even, s_even, y_odd, z_odd, s_odd, gain_slots, gain_sums,
+    ye_s, ye_r, ze_s, ze_r, yo_s, yo_r, zo_s, zo_r,
+    ra_s, ra_r, rb_s, rb_r, gg_s, gg_r, gh_s, gh_r,
+):
+    me = Spot()
+    r, c, z, y = me.r, me.c, me.z, me.y
+    diag = (me.r_x + 1 - 2 * lax.rem(me.r_x, 2), c)
+    chan_peers = [(r, lax.rem(c + d, 8)) for d in range(1, 8)]
+    greet([me.core, me.x, diag] + chan_peers)
+    odd_y = push(odd.at[1 - y], y_odd, (yo_s, yo_r), 0, me.ymate)
+    even_y = [
+        push(even.at[2 * k + 1 - y], y_even.at[k], (ye_s, ye_r), k, me.ymate) for k in range(4)
+    ]
+    g_copies = rows_sum_start(me, gpart, g_mate, (gs1, gr1))
+    even_y[ORDER[0]].start()
+    even_y[ORDER[1]].start()
+    g_cross = rows_sum_cross(me, gpart, g_mate, g_out, g_in, g_copies, (gs2, gr2))
+    o_copies = rows_sum_start(me, opart, o_mate, (os1, or1))
+    o_cross = rows_sum_cross(me, opart, o_mate, o_out, o_in, o_copies, (os2, or2))
+
+    def z_push(k, way):
+        return push(s_even.at[k], z_even.at[k, way], (ze_s, ze_r), 2 * k + way,
+                    me.up if way == 0 else me.dn)
+
+    def odd_push(way):
+        return push(s_odd, z_odd.at[way], (zo_s, zo_r), way, me.up if way == 0 else me.dn)
+
+    def add_even(k):
+        even_y[k].wait_recv()
+        s_even[k] = (even[2 * k + y].astype(F32) + y_even[k].astype(F32)).astype(LOW)
+
+    def hop_even(k):
+        @pl.when(z < k)
+        def _():
+            @pl.when(z > 0)
+            def _():
+                landed(me, z_even.at[k, 0], (ze_s, ze_r), 2 * k + 0)
+                s_even[k] = (s_even[k].astype(F32) + z_even[k, 0].astype(F32)).astype(LOW)
+
+            z_push(k, 0).start()
+
+        @pl.when(z > k)
+        def _():
+            @pl.when(z < 3)
+            def _():
+                landed(me, z_even.at[k, 1], (ze_s, ze_r), 2 * k + 1)
+                s_even[k] = (s_even[k].astype(F32) + z_even[k, 1].astype(F32)).astype(LOW)
+
+            z_push(k, 1).start()
+
+    add_even(ORDER[0])
+    odd_y.start()
+    hop_even(ORDER[0])
+    add_even(ORDER[1])
+    even_y[ORDER[2]].start()
+    hop_even(ORDER[1])
+    odd_y.wait_recv()
+    even_y[ORDER[3]].start()
+    s_odd[...] = (odd[y].astype(F32) + y_odd[...].astype(F32)).astype(LOW)
+
+    @pl.when(z < r)
+    def _():
+        @pl.when(z > 0)
+        def _():
+            landed(me, z_odd.at[0], (zo_s, zo_r), 0)
+            s_odd[...] = (s_odd[...].astype(F32) + z_odd[0].astype(F32)).astype(LOW)
+
+        odd_push(0).start()
+
+    @pl.when(z > r)
+    def _():
+        @pl.when(z < 3)
+        def _():
+            landed(me, z_odd.at[1], (zo_s, zo_r), 1)
+            s_odd[...] = (s_odd[...].astype(F32) + z_odd[1].astype(F32)).astype(LOW)
+
+        odd_push(1).start()
+
+    step = inputs.shape[0] // RS_CHUNKS
+    gain_sum = 0.0
+    for k in range(RS_CHUNKS):
+        rows = pl.ds(k * step, step)
+        grad = rows_sum_chunk(me, gpart, g_mate, g_in, g_copies, g_cross, k)
+        vals = inputs[rows].astype(F32)
+        scale = lax.rsqrt(jnp.mean(vals * vals, axis=-1, keepdims=True) + EPSILON)
+        gain_sum = gain_sum + jnp.sum(grad * vals * scale, axis=0, keepdims=True)
+        pulled = grad * gain[...]
+        inner = jnp.mean(pulled * vals, axis=-1, keepdims=True)
+        ginputs[rows] = (
+            gresid[rows] + scale * pulled - vals * (scale * scale * scale * inner)
+        ).astype(LOW)
+    for k in range(8):
+        lanes = pl.ds(k * 128, 128)
+        gain_slots[0, k, 0:1] = gain_sum[:, k * 128 : (k + 1) * 128]
+        gain_slots[0, k, 1:3] = gains[:, lanes]
+        gain_slots[0, k, 3:8] = jnp.zeros((5, 128), F32)
+    gain_copies = [
+        push(gain_slots.at[0, lax.rem(c + d, 8)], gain_slots.at[1, d], (gg_s, gg_r), d,
+             chan_peers[d - 1])
+        for d in range(1, 8)
+    ]
+    for copy in gain_copies:
+        copy.start()
+
+    add_even(ORDER[2])
+    hop_even(ORDER[2])
+    add_even(ORDER[3])
+    hop_even(ORDER[3])
+
+    for k in range(RS_CHUNKS):
+        rows = pl.ds(k * step, step)
+        total = rows_sum_chunk(me, opart, o_mate, o_in, o_copies, o_cross, k)
+        output[rows] = (resid[rows] + total).astype(LOW)
+
+    shared = gain_slots[0, c]
+    for copy in gain_copies:
+        copy.wait_recv()
+    for d in range(1, 8):
+        shared = shared + gain_slots[1, d]
+    gain_sums[0] = shared
+    row_copies = [
+        push(gain_sums.at[0], gain_sums.at[1 + i], (gh_s, gh_r), i, device)
+        for i, device in enumerate((me.core, me.x, diag))
+    ]
+    for copy in row_copies:
+        copy.start()
+
+    for k in range(4):
+
+        @pl.when(z == k)
+        def _(k=k):
+            @pl.when(z > 0)
+            def _():
+                landed(me, z_even.at[k, 0], (ze_s, ze_r), 2 * k + 0)
+                s_even[k] = (s_even[k].astype(F32) + z_even[k, 0].astype(F32)).astype(LOW)
+
+            @pl.when(z < 3)
+            def _():
+                landed(me, z_even.at[k, 1], (ze_s, ze_r), 2 * k + 1)
+                s_even[k] = (s_even[k].astype(F32) + z_even[k, 1].astype(F32)).astype(LOW)
+
+            even_all[r] = s_even[k]
+
+    even_x = push(even_all.at[r], even_all.at[r], (ra_s, ra_r), 0, me.x)
+    even_c = push(even_all.at[r], even_all.at[r], (ra_s, ra_r), 1, me.core)
+    even_f = push(even_all.at[me.r_x], even_all.at[me.r_x], (ra_s, ra_r), 2, me.core)
+    even_x.start()
+    even_c.start()
+
+    odd_x = push(odd_own, odd_own, (rb_s, rb_r), 0, me.x)
+    odd_c = push(odd_own, odd_own, (rb_s, rb_r), 1, me.core)
+
+    @pl.when(z == r)
+    def _():
+        @pl.when(r > 0)
+        def _():
+            landed(me, z_odd.at[0], (zo_s, zo_r), 0)
+            s_odd[...] = (s_odd[...].astype(F32) + z_odd[0].astype(F32)).astype(LOW)
+
+        @pl.when(r < 3)
+        def _():
+            landed(me, z_odd.at[1], (zo_s, zo_r), 1)
+            s_odd[...] = (s_odd[...].astype(F32) + z_odd[1].astype(F32)).astype(LOW)
+
+        odd_own[...] = s_odd[...]
+        odd_x.start()
+        odd_c.start()
+
+    even_x.wait_recv()
+    even_f.start()
+
+    @pl.when(me.r_x == z)
+    def _():
+        odd_x.wait_recv()
+        odd_c.start()
+
+    @pl.when(jnp.logical_and(z != r, me.r_x != z))
+    def _():
+        odd_c.wait_recv()
+
+    for copy in row_copies:
+        copy.wait()
+    gains_all[...] = gain_sums[0] + gain_sums[1] + gain_sums[2] + gain_sums[3]
+
+    @pl.when(z == r)
+    def _():
+        odd_x.wait_send()
+        odd_c.wait_send()
+
+    @pl.when(me.r_x == z)
+    def _():
+        odd_c.wait_send()
+
+    even_x.wait_send()
+    even_c.wait()
+    even_f.wait()
+    for k in range(4):
+
+        @pl.when(z < k)
+        def _(k=k):
+            z_push(k, 0).wait_send()
+
+        @pl.when(z > k)
+        def _(k=k):
+            z_push(k, 1).wait_send()
+
+    @pl.when(z < r)
+    def _():
+        odd_push(0).wait_send()
+
+    @pl.when(z > r)
+    def _():
+        odd_push(1).wait_send()
+
+    finish_sends(gain_copies + even_y + [odd_y] + g_copies + g_cross + o_copies + o_cross)
+
+
+def final_step(gpart, opart, inputs, resid, gresid, gain, gains, even, odd):
+    sd = jax.ShapeDtypeStruct
+    length, width = inputs.shape
+    scr = (
+        rows_sum_scratch(length, width)
+        + rows_sum_scratch(length, width)
+        + [
+            pltpu.VMEM((4,) + even.shape[1:], LOW),
+            pltpu.VMEM((4, 2) + even.shape[1:], LOW),
+            pltpu.VMEM((4,) + even.shape[1:], LOW),
+            pltpu.VMEM(odd.shape[1:], LOW),
+            pltpu.VMEM((2,) + odd.shape[1:], LOW),
+            pltpu.VMEM(odd.shape[1:], LOW),
+            pltpu.VMEM((2, 8, 8, 128), F32),
+            pltpu.VMEM((4, 8, 128), F32),
+        ]
+        + sem_pair(4) + sem_pair(8) + sem_pair(1) + sem_pair(2)
+        + sem_pair(3) + sem_pair(2) + sem_pair(8) + sem_pair(3)
+    )
+    return pl.pallas_call(
+        final_kernel,
+        name="final_sums",
+        out_shape=[
+            sd(inputs.shape, LOW),
+            sd(inputs.shape, LOW),
+            sd((4,) + even.shape[1:], LOW),
+            sd(odd.shape[1:], LOW),
+            sd((8, 128), F32),
+        ],
+        in_specs=[IN_VMEM] * 9,
+        out_specs=[IN_VMEM] * 5,
+        scratch_shapes=scr,
+        compiler_params=comm_params(6),
+    )(gpart, opart, inputs, resid, gresid, gain, gains, even, odd)
+
+
+def token_masks(starts, first, length, seq_length):
+    where_at = first - 3 + jnp.arange(length + 6, dtype=jnp.int32)
+    tally = jnp.sum((starts[:, None, :] <= where_at[None, :, None]).astype(jnp.int32), axis=2)
+    inside = jnp.logical_and(where_at >= 0, where_at < seq_length)
+    tally = jnp.where(inside[None, :], tally, -1)
+    own = tally[:, 3 : 3 + length]
+    columns = [tally[:, 3 - k : 3 - k + length] == own for k in (1, 2, 3)]
+    columns.append(tally[:, 2 : 2 + length] != own)
+    columns += [tally[:, 3 + k : 3 + k + length] == own for k in (1, 2, 3)]
+    columns.append(jnp.zeros_like(columns[0]))
+    return jnp.stack(columns, axis=2).astype(F32)
+
+
+def pair_diagonal(blocks):
+    side = blocks.shape[1]
+    empty = jnp.zeros((side, side), blocks.dtype)
+    return jnp.concatenate(
+        [jnp.concatenate([blocks[0], empty], 1), jnp.concatenate([empty, blocks[1]], 1)], 0
+    )
+
+
+def split_body(
+    inputs, mix_gain, gate_proj, gate_bias, lift_proj, lift_bias, conv_taps, conv_bias,
+    recur_gate, recur_bias, input_gate, input_bias, decay_param, out_proj, out_bias, mlp_gain,
+    mlp_gate, mlp_up, mlp_down, doc_starts, cotangent,
+):
+    r = lax.axis_index("rows")
+    c = lax.axis_index("chan")
+    length = inputs.shape[0]
+    seq_length = length * 8
+    wide = 2 * GB
+    quarter = mlp_gate.shape[1] // 4
+    rows_f32 = inputs.astype(F32)
+    nrm = rms_scale(rows_f32, mix_gain).astype(LOW)
+    wm = jnp.stack([gate_proj.T, lift_proj.T, out_proj])
+    cut_columns = lambda w: lax.dynamic_slice(w, (0, r * quarter), (w.shape[0], quarter)).T
+    wg, wu, wd = [
+        lax.all_gather(w, "chan", axis=0, tiled=True)
+        for w in (
+            cut_columns(mlp_gate),
+            cut_columns(mlp_up),
+            lax.dynamic_slice(mlp_down, (r * quarter, 0), (quarter, mlp_down.shape[1])),
+        )
+    ]
+    starts = jnp.pad(doc_starts, ((0, 7), (0, 120)))
+    wq, nall, call, halo, starts_all = gather(wm, nrm, cotangent, starts)
+    mask = token_masks(starts_all[:, 0, : doc_starts.shape[1]], c * length, length, seq_length)
+    mine = lambda v: lax.dynamic_slice_in_dim(v, r * wide, wide, axis=v.ndim - 1)
+    decay_own = mine(decay_param)
+    vec = jnp.stack(
+        [mine(gate_bias), mine(lift_bias), mine(conv_bias), mine(recur_bias), mine(input_bias),
+         jax.nn.softplus(-decay_own), jax.nn.sigmoid(-decay_own), jnp.zeros_like(decay_own)]
+    )
+    taps = mine(conv_taps)
+    rgate = pair_diagonal(lax.dynamic_slice_in_dim(recur_gate, 2 * r, 2, 0)).astype(LOW)
+    igate = pair_diagonal(lax.dynamic_slice_in_dim(input_gate, 2 * r, 2, 0)).astype(LOW)
+    gate_pre, lext, conv, rec, opening, a, b, tot = mixer_one(
+        nall, halo, wq, vec, taps, rgate, igate, mask
+    )
+    start = carry_in(tot, False)
+    state, mixed, part = mixer_two(a, b, start, gate_pre, wq)
+    resid, n2all = resid_step(part, inputs, out_bias[None], mlp_gain[None])
+    opart, gpart2, dg, du, dd = mlp(n2all, call, wg, wu, wd)
+    gresid, ball, gains = grad_resid_step(gpart2, cotangent, resid, mlp_gain[None])
+    gate_low, gs, a2, b2, tot2, dwo, gate_sum = mixer_three(
+        ball, wq, gate_pre, state, mixed, rec, vec, mask
+    )
+    carry = carry_in(tot2, True)
+    grad_conv, drg, dig, sums4 = mixer_four(
+        a2, b2, gs, carry, state, start, conv, rec, opening, vec, rgate, igate, mask
+    )
+    head = from_behind(grad_conv[:, :TILE], "chan", -1)
+    gpart, dwg, dwl, sums5 = mixer_five(grad_conv, head, lext, taps, mask, gate_low, nall, wq)
+    vectors = jnp.concatenate([gate_sum, sums5[4:5], sums5[0:4], sums4[3:4], sums4[0:3]], axis=0)
+    small_odd = jnp.pad(
+        vectors.reshape(10, 2, GB).transpose(1, 0, 2).reshape(2, 10 * GB).astype(LOW),
+        ((0, 0), (0, 16 * D - 10 * GB)),
+    ).reshape(2, 16, D)
+    odd = jnp.concatenate(
+        [dwg.reshape(2, GB, D), dwl.reshape(2, GB, D), dwo.reshape(2, GB, D), small_odd], axis=1
+    )
+    blocks = jnp.stack(
+        [jnp.stack([m[:GB, :GB], m[GB:, GB:]]) for m in (drg, dig)]
+    ).reshape(2, 2, 8, GB // 8, GB)
+    small_even = jnp.pad(
+        blocks.transpose(2, 0, 1, 3, 4).reshape(8, 18, D).astype(LOW), ((0, 0), (0, 14), (0, 0))
+    )
+    even = jnp.concatenate([w.reshape(8, quarter, D) for w in (dg, du, dd)] + [small_even], axis=1)
+    output, grad_inputs, even_all, odd_own, gains_all = final_step(
+        gpart, opart, inputs, resid, gresid, mix_gain[None], gains, even, odd
+    )
+    even_all = even_all.astype(F32)
+    odd_own = odd_own.astype(F32)
+    piece = lambda i: even_all[:, i * quarter : (i + 1) * quarter].reshape(4 * quarter, D)
+    gates = even_all[:, 3 * quarter : 3 * quarter + 18].reshape(4, 2, 2, GB // 8, GB)
+    gate_out = lambda i: gates[:, i].reshape(8, GB // 8, GB)
+    own = odd_own[3 * GB :].reshape(-1)[: 10 * GB].reshape(10, GB)
+    return (
+        output, grad_inputs, gains_all[0],
+        odd_own[:GB].T, own[0], odd_own[GB : 2 * GB].T, own[1], own[2:6], own[6],
+        gate_out(0), own[7], gate_out(1), own[8], own[9],
+        odd_own[2 * GB : 3 * GB], gains_all[2], gains_all[1],
+        piece(0).T, piece(1).T, piece(2),
+    )
+
+
 def solution(mesh):
     in_specs = (
         P(("rows", "chan"), None),
@@ -385,4 +1618,5 @@
         P(None, "chan"),
         P("chan", None),
     )
-    return jax.shard_map(body, mesh=mesh, in_specs=in_specs, out_specs=out_specs, check_vma=False)
+    split = mesh.shape["rows"] == 4 and mesh.shape["chan"] == HEADS
+    return jax.shard_map(split_body if split else body, mesh=mesh, in_specs=in_specs, out_specs=out_specs, check_vma=False)

time: 3120 us -> 489 us (0.16)
  waiting for transfers between devices: 2000 us -> 0.11 us
  local copies, waits for them, and re-layouts: 688 us -> 40.1 us
  Pallas kernels: 0 us -> 412 us
  other arithmetic: 153 us -> 16.6 us
  blocking collectives: 126 us -> 0 us
  matrix products: 113 us -> 0 us
    unnamed x9 -> x3, waiting for transfers between devices: 1750 us -> 0.05 us
    pallas_call x0 -> x12, Pallas kernels: none -> 412 us  [the longest x1 157 us: final_step(): pl.pallas_call(final_kernel, name='final_sums', out_shape=[sd(inputs.shap...]
    slice x121 -> x14, local copies, waits for them, and re-layouts: 279 us -> 8.13 us  [the longest x1 2.21 us: split_body(): even_all[:, i * quarter:(i + 1) * quarter].reshape(4 * quarter, D)]
    reshape x28 -> x5, local copies, waits for them, and re-layouts: 161 us -> 7.39 us  [the longest x2 4.63 us: split_body(): even_all[:, i * quarter:(i + 1) * quarter].reshape(4 * quarter, D)]
    psum x1 -> x0, waiting for transfers between devices: 129 us -> none  [body(): summed = lax.psum(shared.reshape(-1), 'rows')]
    all_gather x4 -> x0, blocking collectives: 126 us -> none  [prefix(): pieces = jax.tree.map(lambda part: lax.all_gather(part, axis), value)]
    all_gather x6 -> x3, waiting for transfers between devices: 118 us -> 0.06 us  [split_body(): lax.all_gather(w, 'chan', axis=0, tiled=True)]
    pad x56 -> x2, local copies, waits for them, and re-layouts: 114 us -> 0.64 us  [the longest x1 0.6 us: split_body(): starts = jnp.pad(doc_starts, ((0, 7), (0, 120)))]
  transfers between devices with their start and end apart: 10 -> 4, of which waited for: 5 -> 0; matrix products, arithmetic and copies ran while one was open for 14% -> 6% of each run, Pallas kernels for 0% -> 32%
where the time goes in v1:
time: 489 us; the launch traced here: 485 us
  Pallas kernels  412 us (84%)
  local copies, waits for them, and re-layouts  40.1 us (8%)
  other arithmetic  16.6 us (3%)
  between operations  14.3 us (3%)
    pallas_call x1, Pallas kernels, final_step(): pl.pallas_call(final_kernel, name='final_sums', out_shape=[sd(inputs.shap...  157 us
    pallas_call x1, Pallas kernels, gather(): pl.pallas_call(gather_kernel, name='gather_front', out_shape=[sd((3, 2 *...  79.6 us
    pallas_call x2, Pallas kernels, carry_in(): pl.pallas_call(partial(prefix_kernel, backward), name='carry_back' if bac...  37.8 us
    pallas_call x1, Pallas kernels, grad_resid_step(): pl.pallas_call(grad_resid_kernel, name='grad_resid_sum', out_shape=[sd(co...  32 us
    pallas_call x1, Pallas kernels, resid_step(): pl.pallas_call(resid_kernel, name='resid_sum', out_shape=[sd(inputs.shape...  31 us
    pallas_call x1, Pallas kernels, mlp(): pl.pallas_call(mlp_kernel, name='mlp_both_ways', grid=(blocks,), in_specs...  29.1 us
    pallas_call x1, Pallas kernels, mixer_one(): pl.pallas_call(mixer_one_kernel, name='mixer_forward_gates', grid=(seqs,)...  11.6 us
    pallas_call x1, Pallas kernels, mixer_five(): pl.pallas_call(mixer_five_kernel, name='mixer_backward_conv', grid=(seqs,...  9.9 us
  transfers between devices with their start and end apart: 4, of which 0 were waited for; matrix products, arithmetic and copies ran while one was open for 6% of the time, Pallas kernels for 32%

profile of v1, /device:TPU:0, one launch (start us, length us, event | category | flops | bytes accessed | tf_op | source)
XLA Modules:
  0.0 484.9 jit_solution(10104453061879467129)
XLA Ops:
  9.1 1.4 constant_dynamic-slice_fusion.1
  19.9 79.6 %gather_front.1 = (bf16[3,384,1024]{2,1,0:T(8,128)(2,1)}, bf16[4,256,1024]{2,1,0:T(8,128)(2,1)}, bf16[4,256,1024]{2,1,0:T(8,128)(2,1)}, bf16[4,16,1024]{2,1,0:T(8,128)(2,1)}, s32[4,8,128]{2,1,0:T(8,128)}) custom-call(bf16[3,192,1024]{2,1,0:T(8,128)(2,1)} %pad_maximum_fusion.1.wm, bf16[256,1024]{1,0:T(8,128)(2,1)} %fusion.4.nrm, bf16[256,1024]{1,0:T(8,128)(2,1)} %cot.3, ...), custom_call_target="tpu_custom_call" | custom-call | tf_op jit(solution)/shard_map/gather_front/pallas_call | solution.py:592
  102.6 4.0 stack.102
  112.2 11.6 %mixer_forward_gates.1 = (f32[4,256,384]{2,1,0:T(8,128)}, f32[4,264,384]{2,1,0:T(8,128)}, f32[4,256,384]{2,1,0:T(8,128)}, f32[4,256,384]{2,1,0:T(8,128)}, f32[4,...) custom-call(bf16[4,256,1024]{2,1,0:T(8,128)(2,1)} %get-tuple-element.66.nrm, ...), custom_call_target="tpu_custom_call" | custom-call | tf_op jit(solution)/shard_map/mixer_forward_gates/pallas_call | solution.py:679
  123.8 26.2 %carry_on.1 = f32[4,384]{1,0:T(4,128)} custom-call(f32[4,2,384]{2,1,0:T(2,128)} %get-tuple-element.72.totals), custom_call_target="tpu_custom_call" | custom-call | tf_op jit(solution)/shard_map/carry_on/pallas_call | solution.py:740
  151.2 5.9 %mixer_forward_state.1 = (f32[4,256,384]{2,1,0:T(8,128)}, bf16[4,256,384]{2,1,0:T(8,128)(2,1)}, bf16[4,256,1024]{2,1,0:T(8,128)(2,1)}) custom-call(f32[4,256,384]{2,1,0:T(8,128)} %get-tuple-element.70.a, f32[4,256,384]{2,1,0:T(8,128)} %get-tuple-element.71.b, f32[4,1,384]{2,1,0:T(1,128)} %reshape.142.start, f32[4,256,384]{2,1,0:T(8,128)} %get-tuple-element.73.gate_pre, ...), custom_call_target="tpu_custom_call" | custom-call | tf_op jit(solution)/shard_map/mixer_forward_state/pallas_call | solution.py:770
  157.1 31.0 %resid_sum.1 = (f32[256,1024]{1,0:T(8,128)}, bf16[4,256,1024]{2,1,0:T(8,128)(2,1)}) custom-call(bf16[4,256,1024]{2,1,0:T(8,128)(2,1)} %get-tuple-element.74.part, bf16[256,1024]{1,0:T(8,128)(2,1)} %inputs.3, f32[1,1024]{1,0:T(1,128)} %bitcast.117, f32[1,1024]{1,0:T(1,128)} %bitcast.113), custom_call_target="tpu_custom_call" | custom-call | tf_op jit(solution)/shard_map/resid_sum/pallas_call | solution.py:892
  188.3 29.1 %mlp_both_ways.1 = (bf16[4,256,1024]{2,1,0:T(8,128)(2,1)}, bf16[4,256,1024]{2,1,0:T(8,128)(2,1)}, bf16[768,1024]{1,0:T(8,128)(2,1)}, bf16[768,1024]{1,0:T(8,128)(2,1)}, bf16[768,1024]{1,0:T(8,128)(2,1)}) custom-call(bf16[4,256,1024]{2,1,0:T(8,128)(2,1)} %get-tuple-element.75.nall, bf16[4,256,1024]{2,1,0:T(8,128)(2,1)} %get-tuple-element.76.call, ...), custom_call_target="tpu_custom_call" | custom-call | tf_op jit(solution)/shard_map/mlp_both_ways/pallas_call | solution.py:999
  217.3 32.0 %grad_resid_sum.1 = (f32[256,1024]{1,0:T(8,128)}, bf16[4,256,1024]{2,1,0:T(8,128)(2,1)}, f32[2,1024]{1,0:T(2,128)}) custom-call(bf16[4,256,1024]{2,1,0:T(8,128)(2,1)} %get-tuple-element.77.part, bf16[256,1024]{1,0:T(8,128)(2,1)} %cot.3, f32[256,1024]{1,0:T(8,128)} %get-tuple-element.78.resid, f32[1,1024]{1,0:T(1,128)} %bitcast.114), custom_call_target="tpu_custom_call" | custom-call | tf_op jit(solution)/shard_map/grad_resid_sum/pallas_call | solution.py:938
  249.4 8.9 %mixer_backward_state.1 = (bf16[4,256,384]{2,1,0:T(8,128)(2,1)}, f32[4,256,384]{2,1,0:T(8,128)}, f32[4,256,384]{2,1,0:T(8,128)}, f32[4,256,384]{2,1,0:T(8,128)},...) custom-call(bf16[4,256,1024]{2,1,0:T(8,128)(2,1)} %get-tuple-element.79.ball, ...), custom_call_target="tpu_custom_call" | custom-call | tf_op jit(solution)/shard_map/mixer_backward_state/pallas_call | solution.py:1065
  258.3 11.6 %carry_back.1 = f32[4,384]{1,0:T(4,128)} custom-call(f32[4,2,384]{2,1,0:T(2,128)} %get-tuple-element.86.totals), custom_call_target="tpu_custom_call" | custom-call | tf_op jit(solution)/shard_map/carry_back/pallas_call | solution.py:740
  269.9 1.3 reshape.143.carry_in_ref
  271.2 9.4 %mixer_backward_gates.1 = (f32[4,256,384]{2,1,0:T(8,128)}, f32[384,384]{1,0:T(8,128)}, f32[384,384]{1,0:T(8,128)}, f32[4,384]{1,0:T(4,128)}) custom-call(f32[4,256,384]{2,1,0:T(8,128)} %get-tuple-element.83.a, f32[4,256,384]{2,1,0:T(8,128)} %get-tuple-element.84.b, f32[4,256,384]{2,1,0:T(8,128)} %get-tuple-element.85.gs, ...), custom_call_target="tpu_custom_call" | custom-call | tf_op jit(solution)/shard_map/mixer_backward_gates/pallas_call | solution.py:1134
  282.7 1.5 collective-permute-start
  286.1 4.8 fusion.1.even
  291.6 9.9 %mixer_backward_conv.1 = (bf16[4,256,1024]{2,1,0:T(8,128)(2,1)}, bf16[384,1024]{1,0:T(8,128)(2,1)}, bf16[384,1024]{1,0:T(8,128)(2,1)}, f32[8,384]{1,0:T(8,128)}) custom-call(f32[4,256,384]{2,1,0:T(8,128)} %get-tuple-element.89.grad_conv, f32[4,8,384]{2,1,0:T(8,128)} %copy-done.12, f32[4,264,384]{2,1,0:T(8,128)} %get-tuple-element.90.lext, ...), custom_call_target="tpu_custom_call" | custom-call | tf_op jit(solution)/shard_map/mixer_backward_conv/pallas_call | solution.py:1190
  302.6 2.7 pad_maximum_fusion.odd
  305.3 157.0 %final_sums.1 = (bf16[256,1024]{1,0:T(8,128)(2,1)}, bf16[256,1024]{1,0:T(8,128)(2,1)}, bf16[4,320,1024]{2,1,0:T(8,128)(2,1)}, bf16[592,1024]{1,0:T(8,128)(2,1)}, f32[8,128]{1,0:T(8,128)}) custom-call(bf16[4,256,1024]{2,1,0:T(8,128)(2,1)} %get-tuple-element.92.gpart, bf16[4,256,1024]{2,1,0:T(8,128)(2,1)} %get-tuple-element.93.opart, ...), custom_call_target="tpu_custom_call" | custom-call | tf_op jit(solution)/shard_map/final_sums/pallas_call | solution.py:1452
  462.3 2.1 slice.229
  464.7 1.3 slice_bitcast_fusion
  467.0 2.2 fusion.16
  469.2 1.3 slice_bitcast_fusion.7
  472.2 3.0 copy.194
  475.2 1.6 copy.193
  (119 shorter events, 31.2 us)
Async XLA Ops:
  7.2 1.1 copy-start
  7.2 9.0 %copy-start.16 = (s32[1,8]{1,0:T(1,128)S(1)}, s32[1,8]{1,0:T(1,128)}, u32[]{:S(2)}) copy-start(s32[1,8]{1,0:T(1,128)} %param.40) | copy-start | bytes 100
  7.2 10.4 %copy-start.9 = (bf16[192,1024]{1,0:T(8,128)(2,1)S(1)}, bf16[192,1024]{1,0:T(8,128)(2,1)}, u32[]{:S(2)}) copy-start(bf16[192,1024]{1,0:T(8,128)(2,1)} %param.34) | copy-start | bytes 1179652
  7.2 10.4 %copy-start.10 = (bf16[1024,192]{0,1:T(8,128)(2,1)S(1)}, bf16[1024,192]{0,1:T(8,128)(2,1)}, u32[]{:S(2)}) copy-start(bf16[1024,192]{0,1:T(8,128)(2,1)} %param.25) | copy-start | bytes 1179652
  7.2 10.4 %copy-start.11 = (bf16[1024,192]{0,1:T(8,128)(2,1)S(1)}, bf16[1024,192]{0,1:T(8,128)(2,1)}, u32[]{:S(2)}) copy-start(bf16[1024,192]{0,1:T(8,128)(2,1)} %param.23) | copy-start | bytes 1179652
  7.2 180.9 %all-gather.8.cloned.1.call-start = ((), (), s32[]{:S(2)}) async-start(), calls=%async_computation.2 | async-start | bytes 1769472 | tf_op jit(solution)/shard_map/all_gather | solution.py:1506
  9.0 179.2 %all-gather.6.cloned.1.call-start = ((), (), s32[]{:S(2)}) async-start(), calls=%async_computation.1 | async-start | bytes 1769472 | tf_op jit(solution)/shard_map/all_gather | solution.py:1506
  10.5 8.2 %copy-start.3 = (bf16[256,1024]{1,0:T(8,128)(2,1)S(1)}, bf16[256,1024]{1,0:T(8,128)(2,1)}, u32[]{:S(2)}) copy-start(bf16[256,1024]{1,0:T(8,128)(2,1)} %inputs.3) | copy-start | bytes 1572868
  10.5 8.4 %copy-start.13 = (f32[1024]{0:T(1024)S(1)}, f32[1024]{0:T(1024)}, u32[]{:S(2)}) copy-start(f32[1024]{0:T(1024)} %param.22) | copy-start | bytes 12292
  11.4 176.8 %all-gather.4.cloned.1.call-start = ((), (), s32[]{:S(2)}) async-start(), calls=%async_computation | async-start | bytes 1769472 | tf_op jit(solution)/shard_map/all_gather | solution.py:1506
  280.6 5.5 %copy-start.5 = (bf16[768,1024]{1,0:T(8,128)(2,1)S(1)}, bf16[768,1024]{1,0:T(8,128)(2,1)}, u32[]{:S(2)}) copy-start(bf16[768,1024]{1,0:T(8,128)(2,1)} %get-tuple-element.96) | copy-start | bytes 4718596
  282.7 8.2 %collective-permute-start = (f32[4,8,384]{2,1,0:T(8,128)S(1)}, f32[4,8,384]{2,1,0:T(8,128)S(1)}, u32[]{:S(2)}, u32[]{:S(2)}) collective-permute-start(f32[4,8,384]{2,1,0:T(8,128)S(1)} %slice.167), channel_id=1, source_target_pairs={{1,0},{2,1},{3,2},{4,3},{5,4},{6,5},{7,6},{9,8},{10,9},{11,10},{12... | collective-permute-start | bytes 147464 | tf_op jit(solution)/shard_map/ppermute | solution.py:25
  286.1 4.8 copy-start.15
  286.1 4.8 copy-start.14
  290.9 0.6 copy-start.12
  291.6 11.0 %copy-start.6 = (bf16[384,1024]{1,0:T(8,128)(2,1)S(1)}, bf16[384,1024]{1,0:T(8,128)(2,1)}, u32[]{:S(2)}) copy-start(bf16[384,1024]{1,0:T(8,128)(2,1)} %get-tuple-element.103) | copy-start | bytes 2359300
  462.3 2.1 copy-start.4
  464.7 2.3 copy-start.2
  475.2 1.6 copy-start.8
  475.2 3.2 copy-start.1
  475.2 2.4 copy-start.7
Sparse Core Ops, SparseCore 0:
  10.8 47.2 all-gather.7
  60.9 51.8 all-gather.5
  115.6 44.2 all-gather.3

commit v2 on v0

--- a/solution.py
+++ b/solution.py
@@ -4,6 +4,8 @@
 import jax
 import jax.numpy as jnp
 from jax import lax
+from jax.experimental import pallas as pl
+from jax.experimental.pallas import tpu as pltpu
 from jax.sharding import PartitionSpec as P
 
 D = 1024
@@ -339,6 +341,1353 @@
     )
 
 
+MESH = pl.DeviceIdType.MESH
+LOW = jnp.bfloat16
+F32 = jnp.float32
+VMEM_BYTES = 60 * 2**20
+TILE = 8
+GELU_A = math.sqrt(2.0 / math.pi)
+GELU_B = 0.044715
+
+
+def nt(left, right):
+    return lax.dot_general(left, right, (((1,), (1,)), ((), ())), preferred_element_type=F32)
+
+
+def nn(left, right):
+    return lax.dot_general(left, right, (((1,), (0,)), ((), ())), preferred_element_type=F32)
+
+
+def tn(left, right):
+    return lax.dot_general(left, right, (((0,), (0,)), ((), ())), preferred_element_type=F32)
+
+
+def gelu_pair(values):
+    squared = values * values
+    bend = jnp.tanh(GELU_A * values * (1.0 + GELU_B * squared))
+    half = 0.5 * (1.0 + bend)
+    slope = half + 0.5 * values * (1.0 - bend * bend) * GELU_A * (1.0 + 3.0 * GELU_B * squared)
+    return values * half, slope
+
+
+class Spot:
+    def __init__(self):
+        self.r = lax.axis_index("rows")
+        self.c = lax.axis_index("chan")
+        self.z = lax.div(self.c, 2)
+        self.y = lax.rem(self.c, 2)
+        self.r_core = self.r + 1 - 2 * lax.rem(self.r, 2)
+        self.r_x = lax.rem(self.r + 2, 4)
+        self.core = (self.r_core, self.c)
+        self.x = (self.r_x, self.c)
+        self.c_y = self.c + 1 - 2 * self.y
+        self.ymate = (self.r, self.c_y)
+        self.up = (self.r, lax.rem(self.c + 2, 8))
+        self.dn = (self.r, lax.rem(self.c + 6, 8))
+
+
+def greet(always, maybe=()):
+    barrier = pltpu.get_barrier_semaphore()
+    count = len(always)
+    for device in always:
+        pl.semaphore_signal(barrier, inc=1, device_id=device, device_id_type=MESH)
+    for device, there in maybe:
+
+        @pl.when(there)
+        def _(device=device):
+            pl.semaphore_signal(barrier, inc=1, device_id=device, device_id_type=MESH)
+
+        count = count + jnp.where(there, 1, 0)
+    pl.semaphore_wait(barrier, count)
+
+
+def push(source, target, sems, index, device):
+    return pltpu.make_async_remote_copy(
+        src_ref=source,
+        dst_ref=target,
+        send_sem=sems[0].at[index],
+        recv_sem=sems[1].at[index],
+        device_id=device,
+        device_id_type=MESH,
+    )
+
+
+def landed(me, target, sems, index):
+    push(target, target, sems, index, me.ymate).wait_recv()
+
+
+def sem_pair(count):
+    return [pltpu.SemaphoreType.DMA((count,)), pltpu.SemaphoreType.DMA((count,))]
+
+
+def comm_params(collective_id):
+    return pltpu.CompilerParams(
+        collective_id=collective_id, has_side_effects=True, vmem_limit_bytes=VMEM_BYTES
+    )
+
+
+def plain_params():
+    return pltpu.CompilerParams(
+        dimension_semantics=("arbitrary",), vmem_limit_bytes=VMEM_BYTES
+    )
+
+
+ANYWHERE = pl.BlockSpec(memory_space=pl.ANY)
+IN_VMEM = pl.BlockSpec(memory_space=pltpu.VMEM)
+
+
+def whole(shape):
+    return pl.BlockSpec(shape, lambda s: (0,) * len(shape))
+
+
+def per_seq(shape):
+    return pl.BlockSpec((1,) + shape, lambda s: (s,) + (0,) * len(shape))
+
+
+def decay_terms(rec, softplus_row, reset):
+    log_decay = -8.0 * rec * softplus_row
+    decay = jnp.exp(log_decay)
+    twice = 2.0 * log_decay
+    series = twice * (
+        1.0
+        + twice * (1 / 2 + twice * (1 / 6 + twice * (1 / 24 + twice * (1 / 120 + twice * (1 / 720)))))
+    )
+    gap = jnp.where(twice > -0.25, -series, 1.0 - jnp.exp(twice))
+    return decay, jnp.where(reset, 1.0, jnp.sqrt(gap))
+
+
+def fill_tallies(tallies, starts_row, first, length, seq_length):
+    position = first - 8 + lax.broadcasted_iota(jnp.int32, (length + 16, 1), 0)
+    begun = jnp.sum((starts_row <= position).astype(F32), axis=1, keepdims=True)
+    inside = jnp.logical_and(position >= 0, position < seq_length)
+    tallies[...] = jnp.broadcast_to(jnp.where(inside, begun, -1.0), tallies.shape)
+
+
+def same_document(tallies, length, shift, wide):
+    own = tallies[pl.ds(8, length)]
+    other = tallies[pl.ds(8 + shift, length)]
+    same = (own == other).astype(F32)
+    return jnp.concatenate([same] * (wide // same.shape[1]), axis=1)
+
+
+def pair_diagonal(target, blocks):
+    side = blocks.shape[1]
+    target[...] = jnp.zeros_like(target)
+    target[0:side, 0:side] = blocks[0].astype(target.dtype)
+    target[side : 2 * side, side : 2 * side] = blocks[1].astype(target.dtype)
+
+
+def tile_scan(a, b, backward):
+    row = lax.broadcasted_iota(jnp.int32, a.shape, 1)
+    for step in (1, 2, 4):
+        shift = TILE - step if backward else step
+        there = row < TILE - step if backward else row >= step
+        b = b + a * jnp.where(there, pltpu.roll(b, shift, 1), 0.0)
+        a = a * jnp.where(there, pltpu.roll(a, shift, 1), 1.0)
+    return a, b
+
+
+def carry_start(me, backward, totals, slots, sems):
+    sign = -1 if backward else 1
+    steps = me.c if backward else 7 - me.c
+    copies = [
+        push(totals, slots.at[d], sems, d, (me.r, lax.rem(me.c + 8 + sign * d, 8)))
+        for d in range(1, 8)
+    ]
+    for d in range(1, 8):
+
+        @pl.when(d <= steps)
+        def _(d=d):
+            copies[d - 1].start()
+
+    return copies
+
+
+def carry_join(me, backward, slots, start, sems):
+    behind = 7 - me.c if backward else me.c
+    start[...] = jnp.zeros_like(start)
+    for d in range(7, 0, -1):
+
+        @pl.when(d <= behind)
+        def _(d=d):
+            landed(me, slots.at[d], sems, d)
+            start[...] = slots[d, :, 0] * start[...] + slots[d, :, 1]
+
+
+def carry_sent(me, backward, copies):
+    steps = me.c if backward else 7 - me.c
+    for d in range(1, 8):
+
+        @pl.when(d <= steps)
+        def _(d=d):
+            copies[d - 1].wait_send()
+
+
+def peers_of(me):
+    return [(me.r, lax.rem(me.c + d, 8)) for d in range(1, 8)]
+
+
+class Spread:
+    def __init__(self, me, arrays, pieces, sems):
+        self.me, self.arrays, self.pieces, self.sems = me, arrays, pieces, sems
+        self.go_up = jnp.logical_and(me.z >= me.r, me.z < 3)
+        self.go_dn = jnp.logical_and(me.z <= me.r, me.z > 0)
+        self.source = me.z == me.r
+        self.hop = jnp.where(me.z < me.r, me.r - me.z, me.z - me.r)
+
+    def slab(self, i, k, half):
+        size = self.arrays[i].shape[1] // self.pieces
+        return self.arrays[i].at[half, pl.ds(pl.multiple_of(k * size, 16), size)]
+
+    def copies(self, k):
+        me, found = self.me, []
+        for i in range(len(self.arrays)):
+            piece = self.slab(i, k, me.y)
+            ys, yr, us, ds, zr = self.sems[5 * i : 5 * i + 5]
+            found.append(
+                (
+                    push(piece, piece, (ys, yr), k, me.ymate),
+                    push(piece, piece, (us, zr), k, me.up),
+                    push(piece, piece, (ds, zr), k, me.dn),
+                )
+            )
+        return found
+
+    def send(self, k):
+        found = self.copies(k)
+        for copies in found:
+            copies[0].start()
+
+        @pl.when(self.go_up)
+        def _():
+            for copies in found:
+                copies[1].start()
+
+        @pl.when(self.go_dn)
+        def _():
+            for copies in found:
+                copies[2].start()
+
+    def lead(self, k):
+        @pl.when(self.source)
+        def _():
+            self.send(k)
+
+    def follow(self, k):
+        me = self.me
+        for i in range(len(self.arrays)):
+            us, zr = self.sems[5 * i + 2], self.sems[5 * i + 4]
+            landed(me, self.slab(i, k, me.y), (us, zr), k)
+        self.send(k)
+
+    def step(self, p):
+        if p < self.pieces:
+            self.lead(p)
+        k = p - self.hop
+        there = jnp.logical_and(k >= 0, k < self.pieces)
+
+        @pl.when(jnp.logical_and(there, jnp.logical_not(self.source)))
+        def _():
+            self.follow(lax.rem(k + 2 * self.pieces, self.pieces))
+
+    def arrived(self, k):
+        for i in range(len(self.arrays)):
+            ys, yr = self.sems[5 * i], self.sems[5 * i + 1]
+            landed(self.me, self.slab(i, k, 1 - self.me.y), (ys, yr), k)
+
+    def sent(self, k):
+        found = self.copies(k)
+        for copies in found:
+            copies[0].wait_send()
+
+        @pl.when(self.go_up)
+        def _():
+            for copies in found:
+                copies[1].wait_send()
+
+        @pl.when(self.go_dn)
+        def _():
+            for copies in found:
+                copies[2].wait_send()
+
+    def close(self):
+        @pl.loop(0, self.pieces)
+        def _(k):
+            self.arrived(k)
+            self.sent(k)
+
+
+def spread_sems(arrays, pieces):
+    return [pltpu.SemaphoreType.DMA((pieces,))] * (5 * arrays)
+
+
+class Reduce:
+    def __init__(self, me, parts, mine, from_y, from_z, own, pieces, sems):
+        self.me, self.parts, self.mine = me, parts, mine
+        self.from_y, self.from_z, self.own = from_y, from_z, own
+        self.pieces, self.sems = pieces, sems
+        self.hop = jnp.where(me.z < me.r, me.z, 3 - me.z)
+        self.owner = me.z == me.r
+        self.relays = me.z == me.r_x
+
+    def rows(self, i, k):
+        size = self.mine[i].shape[0] // self.pieces
+        return pl.ds(pl.multiple_of(k * size, 16), size)
+
+    def each(self, k):
+        for i in range(len(self.mine)):
+            yield i, self.rows(i, k), self.sems[11 * i : 11 * i + 11]
+
+    def y_copies(self, k):
+        me = self.me
+        return [
+            push(self.parts[i].at[1 - me.y, rows], self.from_y[i].at[rows], sems[0:2], k, me.ymate)
+            for i, rows, sems in self.each(k)
+        ]
+
+    def y_send(self, k):
+        for copy in self.y_copies(k):
+            copy.start()
+
+    def add(self, i, rows, other):
+        total = self.mine[i][rows].astype(F32) + other[i][rows].astype(F32)
+        self.mine[i][rows] = total.astype(LOW)
+
+    def join(self, k):
+        for i, rows, sems in self.each(k):
+            landed(self.me, self.from_y[i].at[rows], sems[0:2], k)
+            self.add(i, rows, self.from_y)
+
+    def z_copies(self, k, way):
+        found = []
+        for i, rows, sems in self.each(k):
+            target = self.own if way == 2 else self.from_z
+            pair = ((sems[2], sems[4]), (sems[3], sems[4]), (sems[3], sems[5]))[way]
+            found.append(
+                push(self.mine[i].at[rows], target[i].at[rows], pair, k,
+                     self.me.up if way == 0 else self.me.dn)
+            )
+        return found
+
+    def z_way(self, action):
+        me = self.me
+        for way, there in enumerate(
+            (me.z < me.r, me.z > me.r + 1, me.z == me.r + 1)
+        ):
+
+            @pl.when(there)
+            def _(way=way):
+                action(way)
+
+    def chain(self, k):
+        @pl.when(self.hop > 0)
+        def _():
+            for i, rows, sems in self.each(k):
+                landed(self.me, self.from_z[i].at[rows], (sems[2], sems[4]), k)
+                self.add(i, rows, self.from_z)
+
+        def start(way):
+            for copy in self.z_copies(k, way):
+                copy.start()
+
+        self.z_way(start)
+
+    def out_copies(self, k, device, pair):
+        return [
+            push(self.own[i].at[rows], self.own[i].at[rows], sems[pair : pair + 2], k, device)
+            for i, rows, sems in self.each(k)
+        ]
+
+    def finish(self, k):
+        @pl.when(self.me.z > 0)
+        def _():
+            for i, rows, sems in self.each(k):
+                landed(self.me, self.from_z[i].at[rows], (sems[2], sems[4]), k)
+                self.add(i, rows, self.from_z)
+
+        @pl.when(self.me.z < 3)
+        def _():
+            for i, rows, sems in self.each(k):
+                landed(self.me, self.own[i].at[rows], (sems[3], sems[5]), k)
+                self.add(i, rows, self.own)
+
+        for i, rows, sems in self.each(k):
+            self.own[i][rows] = self.mine[i][rows]
+        for copy in self.out_copies(k, self.me.x, 6) + self.out_copies(k, self.me.core, 8):
+            copy.start()
+
+    def relay(self, k):
+        for copy in self.out_copies(k, self.me.x, 6):
+            copy.wait_recv()
+        for copy in self.out_copies(k, self.me.core, 8):
+            copy.start()
+
+    def step(self, p, ahead=2):
+        pieces = self.pieces
+        if p < 0:
+            return
+        if p < pieces:
+            self.join(p)
+            if p + ahead < pieces:
+                self.y_send(p + ahead)
+
+        def there(k):
+            return jnp.logical_and(k >= 0, k < pieces), lax.rem(k + 4 * pieces, pieces)
+
+        if p < pieces + 3:
+            inside, k = there(p - self.hop)
+
+            @pl.when(jnp.logical_and(inside, jnp.logical_not(self.owner)))
+            def _():
+                self.chain(k)
+
+        if 0 <= p - 3 < pieces:
+
+            @pl.when(self.owner)
+            def _():
+                self.finish(p - 3)
+
+        if 0 <= p - 5 < pieces:
+
+            @pl.when(self.relays)
+            def _():
+                self.relay(p - 5)
+
+    def positions(self):
+        return self.pieces + 5
+
+    def close(self):
+        others = jnp.logical_not(jnp.logical_or(self.owner, self.relays))
+
+        @pl.loop(0, self.pieces)
+        def _(k):
+            for copy in self.y_copies(k):
+                copy.wait_send()
+
+            def sent(way):
+                for copy in self.z_copies(k, way):
+                    copy.wait_send()
+
+            self.z_way(sent)
+
+            @pl.when(self.owner)
+            def _():
+                for copy in self.out_copies(k, self.me.x, 6) + self.out_copies(k, self.me.core, 8):
+                    copy.wait_send()
+
+            @pl.when(self.relays)
+            def _():
+                for copy in self.out_copies(k, self.me.core, 8):
+                    copy.wait_send()
+
+            @pl.when(others)
+            def _():
+                for copy in self.out_copies(k, self.me.core, 8):
+                    copy.wait_recv()
+
+
+def reduce_sems(arrays, pieces):
+    return [pltpu.SemaphoreType.DMA((pieces,))] * (11 * arrays)
+
+
+def front_kernel(
+    inputs, cot, gain, vecs, taps_all, rgate_all, igate_all, starts, out_bias, mlp_gain,
+    wm, mg, mu, md,
+    wq_o, wg_o, wu_o, wd_o, nall_o, call, starts_all, gate_o, lext_o, conv_o, rec_o, open_o,
+    state_o, start, mixed_o, resid, n2all,
+    wq, nall, halo, gate_pre, lext, conv, rec, opening, a, b, mixed, part, tot, slots, tallies,
+    rg32, ig32, rgate, igate,
+    mate, out_x, in_x, ms, mr, rxs, rxr, ax, bx, ac, bc,
+    loc, outs, xs, xr, cs, cr, hs, hr, ss, sr, ps, pr, *spread_refs,
+):
+    me = Spot()
+    r, c, z, y = me.r, me.c, me.z, me.y
+    length = inputs.shape[0]
+    seq_length = length * 8
+    wide = taps_all.shape[2]
+    diag = (me.r_x + 1 - 2 * lax.rem(me.r_x, 2), c)
+    barrier = pltpu.get_barrier_semaphore()
+    always = [me.core, me.x, diag] + peers_of(me)
+    for device in always:
+        pl.semaphore_signal(barrier, inc=1, device_id=device, device_id_type=MESH)
+    count = len(always)
+    others = [1, 2, 3]
+    for there, place in ((c < 7, lax.rem(c + 1, 8)), (c > 0, lax.rem(c + 7, 8))):
+        for i in others:
+
+            @pl.when(there)
+            def _(i=i, place=place):
+                pl.semaphore_signal(
+                    barrier, inc=1, device_id=(lax.rem(r + i, 4), place), device_id_type=MESH
+                )
+
+        count = count + jnp.where(there, 3, 0)
+    own = [
+        pltpu.make_async_copy(wm, wq.at[:, y], loc.at[0]),
+        pltpu.make_async_copy(mg, wg_o.at[y], loc.at[1]),
+        pltpu.make_async_copy(mu, wu_o.at[y], loc.at[2]),
+        pltpu.make_async_copy(md, wd_o.at[y], loc.at[3]),
+    ]
+
+    @pl.when(z == r)
+    def _():
+        for copy in own:
+            copy.start()
+
+    heads = [
+        pltpu.make_async_copy(rgate_all.at[pl.ds(2 * r, 2)], rg32, loc.at[4]),
+        pltpu.make_async_copy(igate_all.at[pl.ds(2 * r, 2)], ig32, loc.at[5]),
+    ]
+    for copy in heads:
+        copy.start()
+    here_c = pltpu.make_async_copy(cot, call.at[r], loc.at[6])
+    here_c.start()
+    vals = inputs[...].astype(F32)
+    scale = lax.rsqrt(jnp.mean(vals * vals, axis=-1, keepdims=True) + EPSILON)
+    nall[r] = (vals * scale * gain[...]).astype(LOW)
+    starts_all[r] = starts[...]
+    pl.semaphore_wait(barrier, count)
+
+    x_n = push(nall.at[r], nall.at[r], (xs, xr), 0, me.x)
+    c_n = push(nall.at[r], nall.at[r], (cs, cr), 0, me.core)
+    c_c = push(cot, call.at[r], (cs, cr), 1, me.core)
+    x_c = push(cot, call.at[r], (xs, xr), 1, me.x)
+    fwd_n = push(nall.at[me.r_x], nall.at[me.r_x], (cs, cr), 2, me.core)
+    fwd_c = push(call.at[me.r_x], call.at[me.r_x], (cs, cr), 3, me.core)
+    s_copies = [
+        push(starts_all.at[r], starts_all.at[r], (ss, sr), i, device)
+        for i, device in enumerate((me.core, me.x, diag))
+    ]
+    tail = nall.at[r, pl.ds(length - 16, 16)]
+    halo_copies = [
+        push(tail, halo.at[r], (hs, hr), i, (lax.rem(r + i, 4), lax.rem(c + 1, 8))) for i in range(4)
+    ]
+    glo = [Spread(me, [wq.at[m]], 4, spread_refs[5 * m : 5 * m + 5]) for m in range(3)]
+    pieces = 8
+    mlp_w = Spread(me, [wg_o, wu_o, wd_o], pieces, spread_refs[15:])
+    x_n.start()
+    for copy in s_copies:
+        copy.start()
+
+    @pl.when(c < 7)
+    def _():
+        for copy in halo_copies:
+            copy.start()
+
+    c_n.start()
+    c_c.start()
+
+    @pl.when(c == 0)
+    def _():
+        halo[...] = jnp.zeros_like(halo)
+
+    @pl.when(z == r)
+    def _():
+        own[0].wait()
+
+    for k in range(12):
+        glo[k // 4].lead(k % 4)
+
+        @pl.when(z != r)
+        def _(k=k):
+            glo[k // 4].follow(k % 4)
+
+        if k == 3:
+            for copy in heads:
+                copy.wait()
+            pair_diagonal(rgate, rg32)
+            pair_diagonal(igate, ig32)
+        if k == 7:
+            x_n.wait_recv()
+            fwd_n.start()
+            x_c.start()
+
+    @pl.when(z == r)
+    def _():
+        for copy in own[1:]:
+            copy.wait()
+
+    mlp_w.step(0)
+    for m in range(2):
+        for k in range(4):
+            glo[m].arrived(k)
+    c_n.wait_recv()
+    fwd_n.wait_recv()
+    for copy in s_copies:
+        copy.wait_recv()
+
+    @pl.when(c > 0)
+    def _():
+        for i in range(4):
+            landed(me, halo.at[i], (hs, hr), i)
+
+    vec = vecs.at[r]
+    taps = taps_all.at[r]
+
+    def mixer_one(s):
+        fill_tallies(tallies, starts_all[s, 0:1], c * length, length, seq_length)
+        tokens = nall[s]
+        wgate = wq[0].reshape(wide, tokens.shape[1])
+        wlift = wq[1].reshape(wide, tokens.shape[1])
+        gate_pre[s] = nt(tokens, wgate) + vec[0:1]
+        lifted = nt(tokens, wlift) + vec[1:2]
+        lext[s, 0:8] = (nt(halo[s], wlift) + vec[1:2])[8:16]
+        lext[s, pl.ds(8, length)] = lifted
+        out = vec[2:3] + taps[0:1] * lifted
+        for k in range(1, 4):
+            same = same_document(tallies, length, -k, wide)
+            out = out + taps[k : k + 1] * lext[s, pl.ds(8 - k, length)] * same
+        conv[s] = out
+        low = out.astype(LOW)
+        recur = jax.nn.sigmoid(nn(low, rgate[...]) + vec[3:4])
+        opened = jax.nn.sigmoid(nn(low, igate[...]) + vec[4:5])
+        rec[s] = recur
+        opening[s] = opened
+        reset = same_document(tallies, length, -1, wide) < 0.5
+        decay, scaling = decay_terms(recur, vec[5:6], reset)
+        decay = jnp.where(reset, 0.0, decay)
+        tiles = (length // TILE, TILE, wide)
+        a_scan, b_scan = tile_scan(
+            decay.reshape(tiles), (scaling * opened * out).reshape(tiles), False
+        )
+        a[s] = a_scan.reshape(length, wide)
+        b[s] = b_scan.reshape(length, wide)
+        product = jnp.ones((1, wide), F32)
+        state = jnp.zeros((1, wide), F32)
+        for t in range(length // TILE):
+            last = t * TILE + TILE - 1
+            a_last = a[s, last : last + 1]
+            state = b[s, last : last + 1] + a_last * state
+            product = product * a_last
+        tot[s, 0:1] = product
+        tot[s, 1:2] = state
+
+    for half in range(2):
+
+        @pl.loop(2 * half, 2 * half + 2)
+        def _(s):
+            mixer_one(s)
+
+        mlp_w.step(1 + half)
+
+    carry_copies = carry_start(me, False, tot, slots, (ps, pr))
+    saved = [
+        pltpu.make_async_copy(source, target, outs.at[i])
+        for i, (source, target) in enumerate(
+            ((gate_pre, gate_o), (lext, lext_o), (conv, conv_o), (rec, rec_o), (opening, open_o),
+             (nall, nall_o))
+        )
+    ]
+    for copy in saved:
+        copy.start()
+    x_c.wait_recv()
+    fwd_c.start()
+    for k in range(4):
+        glo[2].arrived(k)
+    save_w = pltpu.make_async_copy(wq, wq_o, outs.at[6])
+    save_w.start()
+    mlp_w.step(3)
+    carry_join(me, False, slots, start, (ps, pr))
+
+    def mixer_two(s):
+        state = start[pl.ds(s, 1)]
+        for t in range(length // TILE):
+            tile = pl.ds(t * TILE, TILE)
+            now = b[s, tile] + a[s, tile] * state
+            b[s, tile] = now
+            state = now[TILE - 1 : TILE]
+        gate_val, _ = gelu_pair(gate_pre[s])
+        mix = (b[s] * gate_val).astype(LOW)
+        mixed[s] = mix
+        part[s] = nn(mix, wq[2].reshape(wide, part.shape[2])).astype(LOW)
+
+    for half in range(2):
+
+        @pl.loop(2 * half, 2 * half + 2)
+        def _(s):
+            mixer_two(s)
+
+        mlp_w.step(4 + half)
+
+    more = [
+        pltpu.make_async_copy(b, state_o, outs.at[7]),
+        pltpu.make_async_copy(mixed, mixed_o, outs.at[8]),
+    ]
+    for copy in more:
+        copy.start()
+    step = length // RS_CHUNKS
+    copies = rows_sum_start(me, part, mate, (ms, mr))
+    crossing = rows_sum_cross(me, part, mate, out_x, in_x, copies, (rxs, rxr))
+    mlp_w.step(6)
+    first = []
+    for k in range(RS_CHUNKS):
+        chunk = pl.ds(k * step, step)
+        total = rows_sum_chunk(me, part, mate, in_x, copies, crossing, k)
+        res = inputs[chunk].astype(F32) + total + out_bias[...]
+        resid[chunk] = res
+        scale = lax.rsqrt(jnp.mean(res * res, axis=-1, keepdims=True) + EPSILON)
+        n2all[r, chunk] = (res * scale * mlp_gain[...]).astype(LOW)
+        first.append(spread_chunk(me, n2all, k, (ax, bx), (ac, bc)))
+        if k % 2 == 1:
+            mlp_w.step(7 + k // 2)
+    mlp_w.step(9)
+    mlp_w.step(10)
+    spread_rest(me, n2all, first, (ac, bc))
+    finish_sends(copies + crossing)
+    mlp_w.close()
+    for m in range(3):
+        for k in range(4):
+            glo[m].sent(k)
+    x_n.wait_send()
+    x_c.wait_send()
+    c_n.wait_send()
+    c_c.wait()
+    fwd_n.wait_send()
+    fwd_c.wait()
+    finish_sends(s_copies)
+
+    @pl.when(c < 7)
+    def _():
+        finish_sends(halo_copies)
+
+    carry_sent(me, False, carry_copies)
+    here_c.wait()
+    for copy in saved + [save_w] + more:
+        copy.wait()
+
+
+def front(inputs, cot, gain, vecs, taps_all, rgate_all, igate_all, starts, out_bias, mlp_gain,
+          wm, mg, mu, md):
+    length, width = inputs.shape
+    wide = 2 * wm.shape[1]
+    hidden = mg.shape[1]
+    sd = jax.ShapeDtypeStruct
+    tall = sd((4, length, wide), F32)
+    ext = sd((4, length + 8, wide), F32)
+    low = sd((4, length, wide), LOW)
+    tokens = sd((4, length, width), LOW)
+    vmem = lambda spec: pltpu.VMEM(spec.shape, spec.dtype)
+    outs = [
+        (sd((3, 2, wide // 2, width), LOW), ANYWHERE),
+        (sd((2, width, hidden), LOW), ANYWHERE),
+        (sd((2, width, hidden), LOW), ANYWHERE),
+        (sd((2, hidden, width), LOW), ANYWHERE),
+        (tokens, ANYWHERE),
+        (tokens, ANYWHERE),
+        (sd((4,) + starts.shape, starts.dtype), IN_VMEM),
+        (tall, ANYWHERE),
+        (ext, ANYWHERE),
+        (tall, ANYWHERE),
+        (tall, ANYWHERE),
+        (tall, ANYWHERE),
+        (tall, ANYWHERE),
+        (sd((4, wide), F32), IN_VMEM),
+        (low, ANYWHERE),
+        (sd((length, width), F32), IN_VMEM),
+        (tokens, IN_VMEM),
+    ]
+    dma = pltpu.SemaphoreType.DMA
+    return pl.pallas_call(
+        front_kernel,
+        name="front",
+        out_shape=[o[0] for o in outs],
+        in_specs=[IN_VMEM, ANYWHERE] + [IN_VMEM] * 3 + [ANYWHERE] * 2 + [IN_VMEM] * 3 + [ANYWHERE] * 4,
+        out_specs=[o[1] for o in outs],
+        scratch_shapes=[
+            pltpu.VMEM((3, 2, wide // 2, width), LOW), vmem(tokens), pltpu.VMEM((4, 16, width), LOW),
+            vmem(tall), vmem(ext), vmem(tall), vmem(tall), vmem(tall), vmem(tall), vmem(tall),
+            vmem(low), vmem(tokens), pltpu.VMEM((4, 2, wide), F32), pltpu.VMEM((8, 4, 2, wide), F32),
+            pltpu.VMEM((length + 16, 128), F32),
+            pltpu.VMEM((2, GB, GB), F32), pltpu.VMEM((2, GB, GB), F32),
+            pltpu.VMEM((wide, wide), LOW), pltpu.VMEM((wide, wide), LOW),
+        ]
+        + rows_sum_scratch(length, width) + sem_pair(RS_CHUNKS) + sem_pair(2 * RS_CHUNKS)
+        + [dma((7,)), dma((9,))] + sem_pair(2) + sem_pair(4) + sem_pair(4) + sem_pair(3)
+        + sem_pair(8) + spread_sems(3, 4) + spread_sems(3, 8),
+        compiler_params=comm_params(1),
+    )(inputs, cot, gain, vecs, taps_all, rgate_all, igate_all, starts, out_bias, mlp_gain,
+      wm, mg, mu, md)
+
+
+RS_CHUNKS = 4
+
+
+def rows_sum_start(me, part, mate, sems):
+    length = part.shape[1]
+    step = length // RS_CHUNKS
+    far = lax.rem(me.r_core + 2, 4)
+    copies = []
+    for block, owner in enumerate((far, me.r_core)):
+        for k in range(RS_CHUNKS):
+            rows = pl.ds(k * step, step)
+            copies.append(
+                push(part.at[owner, rows], mate.at[block, rows], sems, block * RS_CHUNKS + k, me.core)
+            )
+    for copy in copies:
+        copy.start()
+    return copies
+
+
+def rows_sum_cross(me, part, mate, out_x, in_x, copies, sems):
+    length = part.shape[1]
+    step = length // RS_CHUNKS
+    crossing = []
+    for k in range(RS_CHUNKS):
+        rows = pl.ds(k * step, step)
+        copies[k].wait_recv()
+        out_x[rows] = (part[me.r_x, rows].astype(F32) + mate[0, rows].astype(F32)).astype(LOW)
+        copy = push(out_x.at[rows], in_x.at[rows], sems, k, me.x)
+        copy.start()
+        crossing.append(copy)
+    return crossing
+
+
+def rows_sum_chunk(me, part, mate, in_x, copies, crossing, k):
+    length = part.shape[1]
+    step = length // RS_CHUNKS
+    rows = pl.ds(k * step, step)
+    copies[RS_CHUNKS + k].wait_recv()
+    crossing[k].wait_recv()
+    return part[me.r, rows].astype(F32) + mate[1, rows].astype(F32) + in_x[rows].astype(F32)
+
+
+def finish_sends(copies):
+    for copy in copies:
+        copy.wait_send()
+
+
+def rows_sum_scratch(length, width):
+    return [
+        pltpu.VMEM((2, length, width), LOW),
+        pltpu.VMEM((length, width), LOW),
+        pltpu.VMEM((length, width), LOW),
+    ] + sem_pair(2 * RS_CHUNKS) + sem_pair(RS_CHUNKS)
+
+
+def spread_chunk(me, all_ref, k, sems_x, sems_c):
+    length = all_ref.shape[1]
+    step = length // RS_CHUNKS
+    rows = pl.ds(k * step, step)
+    mine = all_ref.at[me.r, rows]
+    copies = [
+        push(mine, mine, sems_x, k, me.x),
+        push(mine, mine, sems_c, k, me.core),
+    ]
+    for copy in copies:
+        copy.start()
+    return copies
+
+
+def spread_rest(me, all_ref, first, sems_c):
+    length = all_ref.shape[1]
+    step = length // RS_CHUNKS
+    passed = []
+    for k in range(RS_CHUNKS):
+        first[k][0].wait_recv()
+        theirs = all_ref.at[me.r_x, pl.ds(k * step, step)]
+        copy = push(theirs, theirs, sems_c, RS_CHUNKS + k, me.core)
+        copy.start()
+        passed.append(copy)
+    for k in range(RS_CHUNKS):
+        first[k][0].wait_send()
+        first[k][1].wait()
+        passed[k].wait()
+
+
+def mlp_kernel(
+    nall, call, wg, wu, wd, part, gpart, dg_o, du_o, dd_o,
+    acc_out, acc_in, acc_g, acc_u, acc_d,
+):
+    block = pl.program_id(0)
+    length = nall.shape[1]
+
+    @pl.when(block == 0)
+    def _():
+        acc_out[...] = jnp.zeros_like(acc_out)
+        acc_in[...] = jnp.zeros_like(acc_in)
+
+    acc_g[...] = jnp.zeros_like(acc_g)
+    acc_u[...] = jnp.zeros_like(acc_u)
+    acc_d[...] = jnp.zeros_like(acc_d)
+
+    @pl.loop(0, nall.shape[0])
+    def _(s):
+        tokens = nall[s]
+        cot = call[s]
+        gate = nn(tokens, wg[0])
+        up = nn(tokens, wu[0])
+        grad_hidden = nt(cot, wd[0])
+        gate_val, slope = gelu_pair(gate)
+        hidden = (gate_val * up).astype(LOW)
+        grad_gate = (grad_hidden * up * slope).astype(LOW)
+        grad_up = (grad_hidden * gate_val).astype(LOW)
+        acc_out[s] += nn(hidden, wd[0])
+        acc_in[s] += nt(grad_gate, wg[0]) + nt(grad_up, wu[0])
+        acc_d[...] += tn(hidden, cot)
+        acc_g[...] += tn(tokens, grad_gate)
+        acc_u[...] += tn(tokens, grad_up)
+
+    dg_o[0] = acc_g[...].astype(LOW)
+    du_o[0] = acc_u[...].astype(LOW)
+    dd_o[0] = acc_d[...].astype(LOW)
+
+    @pl.when(block == pl.num_programs(0) - 1)
+    def _():
+        part[...] = acc_out[...].astype(LOW)
+        gpart[...] = acc_in[...].astype(LOW)
+
+
+def mlp(nall, call, wg, wu, wd):
+    blocks, width, hidden = wg.shape
+    sd = jax.ShapeDtypeStruct
+    inward = pl.BlockSpec((1, width, hidden), lambda h: (h, 0, 0))
+    outward = pl.BlockSpec((1, hidden, width), lambda h: (h, 0, 0))
+    return pl.pallas_call(
+        mlp_kernel,
+        name="mlp_both_ways",
+        grid=(blocks,),
+        in_specs=[whole(nall.shape), whole(call.shape), inward, inward, outward],
+        out_specs=[whole(nall.shape), whole(nall.shape), inward, inward, outward],
+        out_shape=[sd(nall.shape, LOW)] * 2 + [sd(w.shape, LOW) for w in (wg, wu, wd)],
+        scratch_shapes=[pltpu.VMEM(nall.shape, F32)] * 2
+        + [pltpu.VMEM(w.shape[1:], F32) for w in (wg, wu, wd)],
+        compiler_params=plain_params(),
+    )(nall, call, wg, wu, wd)
+
+
+def back_kernel(
+    gpart2, cot, resid, inputs, mlp_gain, mix_gain, vecs, taps_all, starts_all, start,
+    opart, dmg, dmu, dmd, wq_h, nall_h, gate_h, lext_h, conv_h, rec_h, open_h, state_h, mixed_h,
+    rgate_all, igate_all,
+    output, ginputs, own_g, own_u, own_d, own_e, own_l, gates_all, gains_all,
+    wq, nall, gate_pre, lext, conv, rec, opening, state, mixed, a, b, gconv, heads_in,
+    gate_low, ball, gresid, opart_v, acc_a, acc_b, acc_r, acc_i, sums, prev_ext,
+    early, late, mine_g, mine_u, mine_d, y_g, y_u, y_d, y_e, y_l,
+    z_g, z_u, z_d, z_e, z_l,
+    tot, slots, carry, tallies, rg32, ig32, rgate, igate,
+    gate_send, gate_slots, gain_slots, gain_sums,
+    mate, out_x, in_x, ms, mr, rxs, rxr, o_mate, o_out, o_in, oms, omr, oxs, oxr,
+    nms, nmr, nxs, nxr, ax, bx, ac, bc,
+    loc, ps, pr, hs, hr, ggs, ggr, ghs, ghr, qs, qr, ts, tr, *reduce_refs,
+):
+    me = Spot()
+    r, c, z, y = me.r, me.c, me.z, me.y
+    length = inputs.shape[0]
+    seq_length = length * 8
+    wide = taps_all.shape[2]
+    width = inputs.shape[1]
+    side = wide // 2
+    step = length // RS_CHUNKS
+    diag = (me.r_x + 1 - 2 * lax.rem(me.r_x, 2), c)
+    chan_peers = peers_of(me)
+    row_peers = (me.core, me.x, diag)
+    loads = [
+        pltpu.make_async_copy(source, target, loc.at[i])
+        for i, (source, target) in enumerate(
+            (
+                (dmg.at[y], mine_g), (dmu.at[y], mine_u), (dmd.at[y], mine_d),
+                (gate_h, gate_pre), (state_h, state), (mixed_h, mixed), (rec_h, rec), (wq_h, wq),
+                (open_h, opening), (conv_h, conv), (lext_h, lext), (nall_h, nall),
+                (opart, opart_v), (rgate_all.at[pl.ds(2 * r, 2)], rg32),
+                (igate_all.at[pl.ds(2 * r, 2)], ig32),
+            )
+        )
+    ]
+    for copy in loads:
+        copy.start()
+    greet(list(row_peers) + chan_peers)
+    n_mlp = 11 * 3
+    big = Reduce(me, [dmg, dmu, dmd], [mine_g, mine_u, mine_d], [y_g, y_u, y_d], [z_g, z_u, z_d],
+                 [own_g, own_u, own_d], 8, reduce_refs[:n_mlp])
+    mid = Reduce(me, [early], [early.at[y]], [y_e], [z_e], [own_e], 4, reduce_refs[n_mlp : n_mlp + 11])
+    end = Reduce(me, [late], [late.at[y]], [y_l], [z_l], [own_l], 7, reduce_refs[n_mlp + 11 :])
+
+    copies = rows_sum_start(me, gpart2, mate, (ms, mr))
+    big.y_send(0)
+    big.y_send(1)
+    crossing = rows_sum_cross(me, gpart2, mate, out_x, in_x, copies, (rxs, rxr))
+    for copy in loads[:3]:
+        copy.wait()
+    big.step(0)
+    first = []
+    gain2_sum = 0.0
+    bias_sum = 0.0
+    for k in range(RS_CHUNKS):
+        rows = pl.ds(k * step, step)
+        grad = rows_sum_chunk(me, gpart2, mate, in_x, copies, crossing, k)
+        res = resid[rows]
+        scale = lax.rsqrt(jnp.mean(res * res, axis=-1, keepdims=True) + EPSILON)
+        gain2_sum = gain2_sum + jnp.sum(grad * res * scale, axis=0, keepdims=True)
+        pulled = grad * mlp_gain[...]
+        inner = jnp.mean(pulled * res, axis=-1, keepdims=True)
+        total = cot[rows].astype(F32) + scale * pulled - res * (scale * scale * scale * inner)
+        bias_sum = bias_sum + jnp.sum(total, axis=0, keepdims=True)
+        gresid[rows] = total
+        ball[r, rows] = total.astype(LOW)
+        first.append(spread_chunk(me, ball, k, (ax, bx), (ac, bc)))
+        if k % 2 == 1:
+            big.step(1 + k // 2)
+    for copy in loads[3:]:
+        copy.wait()
+    pair_diagonal(rgate, rg32)
+    pair_diagonal(igate, ig32)
+    big.step(3)
+    spread_rest(me, ball, first, (ac, bc))
+    finish_sends(copies + crossing)
+
+    vec = vecs.at[r]
+    taps = taps_all.at[r]
+    acc_a[...] = jnp.zeros_like(acc_a)
+    acc_b[...] = jnp.zeros_like(acc_b)
+    acc_r[...] = jnp.zeros_like(acc_r)
+    acc_i[...] = jnp.zeros_like(acc_i)
+    sums[...] = jnp.zeros_like(sums)
+
+    def reset_of(s):
+        fill_tallies(tallies, starts_all[s, 0:1], c * length, length, seq_length)
+        return same_document(tallies, length, -1, wide) < 0.5
+
+    def mixer_three(s):
+        branch = ball[s]
+        grad_mixed = nt(branch, wq[2].reshape(wide, width))
+        gate_val, slope = gelu_pair(gate_pre[s])
+        grad_gate = grad_mixed * state[s] * slope
+        low = grad_gate.astype(LOW)
+        gate_low[s] = low
+        sums[0:1] += jnp.sum(grad_gate, axis=0, keepdims=True)
+        acc_a[...] += tn(mixed[s], branch)
+        acc_b[...] += tn(low, nall[s])
+        grad_state = grad_mixed * gate_val
+        gate_pre[s] = grad_state
+        decay = jnp.where(reset_of(s), 0.0, jnp.exp(-8.0 * rec[s] * vec[5:6]))
+        tiles = (length // TILE, TILE, wide)
+        a_scan, b_scan = tile_scan(
+            decay.reshape(tiles), (decay * grad_state).reshape(tiles), True
+        )
+        a[s] = a_scan.reshape(length, wide)
+        b[s] = b_scan.reshape(length, wide)
+        product = jnp.ones((1, wide), F32)
+        carried = jnp.zeros((1, wide), F32)
+        for t in range(length // TILE - 1, -1, -1):
+            head = t * TILE
+            a_head = a[s, head : head + 1]
+            carried = b[s, head : head + 1] + a_head * carried
+            product = product * a_head
+        tot[s, 0:1] = product
+        tot[s, 1:2] = carried
+
+    for half in range(2):
+
+        @pl.loop(2 * half, 2 * half + 2)
+        def _(s):
+            mixer_three(s)
+
+        if half == 0:
+            big.step(4)
+
+    carry_copies = carry_start(me, True, tot, slots, (ps, pr))
+    for j in range(2):
+        early[j, 0:side] = acc_a[j * side : (j + 1) * side].astype(LOW)
+        early[j, side : 2 * side] = acc_b[j * side : (j + 1) * side].astype(LOW)
+    acc_b[...] = jnp.zeros_like(acc_b)
+    big.step(5)
+    carry_join(me, True, slots, carry, (ps, pr))
+
+    def mixer_four(s):
+        now = carry[pl.ds(s, 1)]
+        gconv[s, pl.ds(length, TILE)] = jnp.broadcast_to(now, (TILE, wide))
+        for t in range(length // TILE - 1, -1, -1):
+            rows = pl.ds(t * TILE, TILE)
+            moved = b[s, rows] + a[s, rows] * now
+            gconv[s, rows] = moved
+            now = moved[0:1]
+        carried = gate_pre[s] + gconv[s, pl.ds(1, length)]
+        prev_ext[0:TILE] = jnp.broadcast_to(start[pl.ds(s, 1)], (TILE, wide))
+        prev_ext[pl.ds(TILE, length)] = state[s]
+        previous = prev_ext[pl.ds(TILE - 1, length)]
+        recur, opened, conv_s = rec[s], opening[s], conv[s]
+        reset = reset_of(s)
+        decay, scaling = decay_terms(recur, vec[5:6], reset)
+        pulled = carried * scaling
+        grad_opening = pulled * conv_s
+        grad_log = carried * (previous * decay - opened * conv_s * (decay * decay / scaling))
+        grad_log = jnp.where(reset, 0.0, grad_log)
+        grad_rec = grad_log * (-8.0 * vec[5:6])
+        grad_rpre = grad_rec * recur * (1.0 - recur)
+        grad_opre = grad_opening * opened * (1.0 - opened)
+        r_low, o_low, conv_low = grad_rpre.astype(LOW), grad_opre.astype(LOW), conv_s.astype(LOW)
+        total = pulled * opened + nt(r_low, rgate[...]) + nt(o_low, igate[...])
+        gconv[s, 0:length] = total
+        acc_r[...] += tn(conv_low, r_low)
+        acc_i[...] += tn(conv_low, o_low)
+        sums[7:8] += jnp.sum(grad_rpre, axis=0, keepdims=True)
+        sums[8:9] += jnp.sum(grad_opre, axis=0, keepdims=True)
+        sums[9:10] += jnp.sum(grad_log * recur, axis=0, keepdims=True) * (8.0 * vec[6:7])
+        sums[6:7] += jnp.sum(total, axis=0, keepdims=True)
+
+    for half in range(2):
+
+        @pl.loop(2 * half, 2 * half + 2)
+        def _(s):
+            mixer_four(s)
+
+        if half == 0:
+            big.step(6)
+            mid.y_send(0)
+            mid.y_send(1)
+
+    heads = [
+        push(gconv.at[s, pl.ds(0, TILE)], heads_in.at[s], (hs, hr), s, (r, lax.rem(c + 7, 8)))
+        for s in range(4)
+    ]
+
+    @pl.when(c > 0)
+    def _():
+        for copy in heads:
+            copy.start()
+
+    @pl.when(c == 7)
+    def _():
+        heads_in[...] = jnp.zeros_like(heads_in)
+
+    cut = side // 8
+    for k in range(8):
+        at = k * cut
+        gate_send[k] = jnp.concatenate(
+            [m[j * side + at : j * side + at + cut, j * side : (j + 1) * side]
+             for m in (acc_r, acc_i) for j in range(2)], axis=0
+        ).astype(LOW)
+    gate_copies = [
+        push(gate_send.at[lax.rem(c + d, 8)], gate_slots.at[d], (qs, qr), d, chan_peers[d - 1])
+        for d in range(1, 8)
+    ]
+    for copy in gate_copies:
+        copy.start()
+    big.step(7)
+
+    @pl.when(c < 7)
+    def _():
+        for s in range(4):
+            landed(me, heads_in.at[s], (hs, hr), s)
+
+    def mixer_five(s):
+        fill_tallies(tallies, starts_all[s, 0:1], c * length, length, seq_length)
+        grad = gconv[s, 0:length]
+        prev_ext[0:length] = grad
+        prev_ext[pl.ds(length, TILE)] = heads_in[s]
+        grad_lifted = taps[0:1] * grad
+        sums[2:3] += jnp.sum(grad * lext[s, pl.ds(TILE, length)], axis=0, keepdims=True)
+        for k in range(1, 4):
+            ahead = prev_ext[pl.ds(k, length)] * same_document(tallies, length, k, wide)
+            grad_lifted = grad_lifted + taps[k : k + 1] * ahead
+            behind = lext[s, pl.ds(TILE - k, length)] * same_document(tallies, length, -k, wide)
+            sums[2 + k : 3 + k] += jnp.sum(grad * behind, axis=0, keepdims=True)
+        sums[1:2] += jnp.sum(grad_lifted, axis=0, keepdims=True)
+        lift_low = grad_lifted.astype(LOW)
+        acc_b[...] += tn(lift_low, nall[s])
+        ball[s] = (
+            nn(gate_low[s], wq[0].reshape(wide, width)) + nn(lift_low, wq[1].reshape(wide, width))
+        ).astype(LOW)
+
+    for half in range(2):
+
+        @pl.loop(2 * half, 2 * half + 2)
+        def _(s):
+            mixer_five(s)
+
+        if half == 0:
+            big.step(8)
+            mid.step(0)
+
+    n_copies = rows_sum_start(me, ball, mate, (nms, nmr))
+    late[...] = jnp.zeros_like(late)
+    for j in range(2):
+        late[j, 0:side] = acc_b[j * side : (j + 1) * side].astype(LOW)
+        late[j, side : side + 16, 0:side] = sums[:, j * side : (j + 1) * side].astype(LOW)
+    end.y_send(0)
+    end.y_send(1)
+    end.y_send(2)
+    n_cross = rows_sum_cross(me, ball, mate, out_x, in_x, n_copies, (nxs, nxr))
+    o_copies = rows_sum_start(me, opart_v, o_mate, (oms, omr))
+    o_cross = rows_sum_cross(me, opart_v, o_mate, o_out, o_in, o_copies, (oxs, oxr))
+    big.step(9)
+    mid.step(1)
+    big.step(10)
+    mid.step(2)
+    gain_sum = 0.0
+    for k in range(RS_CHUNKS):
+        rows = pl.ds(k * step, step)
+        grad = rows_sum_chunk(me, ball, mate, in_x, n_copies, n_cross, k)
+        vals = inputs[rows].astype(F32)
+        scale = lax.rsqrt(jnp.mean(vals * vals, axis=-1, keepdims=True) + EPSILON)
+        gain_sum = gain_sum + jnp.sum(grad * vals * scale, axis=0, keepdims=True)
+        pulled = grad * mix_gain[...]
+        inner = jnp.mean(pulled * vals, axis=-1, keepdims=True)
+        ginputs[rows] = (
+            gresid[rows] + scale * pulled - vals * (scale * scale * scale * inner)
+        ).astype(LOW)
+        if k == 1:
+            big.step(11)
+            mid.step(3)
+    for k in range(8):
+        lanes = slice(k * 128, (k + 1) * 128)
+        gain_slots[0, k] = jnp.concatenate(
+            [gain_sum[:, lanes], gain2_sum[:, lanes], bias_sum[:, lanes], jnp.zeros((5, 128), F32)], 0
+        )
+    gain_copies = [
+        push(gain_slots.at[0, lax.rem(c + d, 8)], gain_slots.at[1, d], (ggs, ggr), d,
+             chan_peers[d - 1])
+        for d in range(1, 8)
+    ]
+    for copy in gain_copies:
+        copy.start()
+    big.step(12)
+    for p in range(3):
+        end.step(p, 3)
+    mid.step(4)
+    for k in range(RS_CHUNKS):
+        rows = pl.ds(k * step, step)
+        total = rows_sum_chunk(me, opart_v, o_mate, o_in, o_copies, o_cross, k)
+        output[rows] = (resid[rows] + total).astype(LOW)
+    for p in range(3, 6):
+        end.step(p, 3)
+    mid.step(5)
+    gate_total = gate_send[c].astype(F32)
+    for d in range(1, 8):
+        gate_copies[d - 1].wait_recv()
+        gate_total = gate_total + gate_slots[d].astype(F32)
+    gates_all[r] = gate_total.astype(LOW)
+    gate_rows = [
+        push(gates_all.at[r], gates_all.at[r], (ts, tr), i, device)
+        for i, device in enumerate(row_peers)
+    ]
+    for copy in gate_rows:
+        copy.start()
+    shared = gain_slots[0, c]
+    for d in range(1, 8):
+        gain_copies[d - 1].wait_recv()
+        shared = shared + gain_slots[1, d]
+    gain_sums[0] = shared
+    row_copies = [
+        push(gain_sums.at[0], gain_sums.at[1 + i], (ghs, ghr), i, device)
+        for i, device in enumerate(row_peers)
+    ]
+    for copy in row_copies:
+        copy.start()
+    end.step(6, 3)
+    mid.step(6)
+    for p in range(7, end.positions()):
+        end.step(p, 3)
+        mid.step(p)
+    for copy in row_copies + gate_rows:
+        copy.wait()
+    gains_all[...] = gain_sums[0] + gain_sums[1] + gain_sums[2] + gain_sums[3]
+
+    @pl.when(c > 0)
+    def _():
+        finish_sends(heads)
+
+    finish_sends(gain_copies + gate_copies + n_copies + n_cross + o_copies + o_cross)
+    carry_sent(me, True, carry_copies)
+    big.close()
+    mid.close()
+    end.close()
+
+
+def back(gpart2, cot, resid, inputs, mlp_gain, mix_gain, vecs, taps_all, starts_all, start,
+         opart, dmg, dmu, dmd, wq, nall, gate_pre, lext, conv, rec, opening, state, mixed,
+         rgate_all, igate_all):
+    length, width = inputs.shape
+    wide = taps_all.shape[2]
+    side = wide // 2
+    sd = jax.ShapeDtypeStruct
+    vmem = pltpu.VMEM
+    dma = pltpu.SemaphoreType.DMA
+    like = lambda v: vmem(v.shape, v.dtype)
+    shard = lambda v: vmem(v.shape[1:], LOW)
+    tall = vmem((4, length, wide), F32)
+    early, late = (2, 2 * side, width), (2, side + 32, width)
+    odd = lambda: [shard(dmg), shard(dmu), shard(dmd), vmem(early[1:], LOW), vmem(late[1:], LOW)]
+    outs = [
+        sd(inputs.shape, LOW), sd(inputs.shape, LOW),
+        sd(dmg.shape[1:], LOW), sd(dmu.shape[1:], LOW), sd(dmd.shape[1:], LOW),
+        sd(early[1:], LOW), sd(late[1:], LOW), sd((4, side // 2, side), LOW), sd((8, 128), F32),
+    ]
+    return pl.pallas_call(
+        back_kernel,
+        name="back",
+        out_shape=outs,
+        in_specs=[IN_VMEM] * 10 + [ANYWHERE] * 15,
+        out_specs=[IN_VMEM] * len(outs),
+        scratch_shapes=[
+            like(wq), like(nall), tall, like(lext), tall, tall, tall, tall, like(mixed),
+            tall, tall, vmem((4, length + TILE, wide), F32), vmem((4, TILE, wide), F32),
+            vmem((4, length, wide), LOW), like(gpart2), vmem((length, width), F32), like(opart),
+            vmem((wide, width), F32), vmem((wide, width), F32),
+            vmem((wide, wide), F32), vmem((wide, wide), F32), vmem((16, wide), F32),
+            vmem((length + TILE, wide), F32),
+            vmem(early, LOW), vmem(late, LOW),
+        ]
+        + odd()[:3] + odd() + odd()
+        + [
+            vmem((4, 2, wide), F32), vmem((8, 4, 2, wide), F32), vmem((4, wide), F32),
+            vmem((length + 16, 128), F32), vmem((2, GB, GB), F32), vmem((2, GB, GB), F32),
+            vmem((wide, wide), LOW), vmem((wide, wide), LOW),
+            vmem((8, side // 2, side), LOW), vmem((8, side // 2, side), LOW),
+            vmem((2, 8, 8, 128), F32), vmem((4, 8, 128), F32),
+        ]
+        + rows_sum_scratch(length, width) + rows_sum_scratch(length, width)
+        + sem_pair(2 * RS_CHUNKS) + sem_pair(RS_CHUNKS)
+        + sem_pair(RS_CHUNKS) + sem_pair(2 * RS_CHUNKS)
+        + [dma((15,))] + sem_pair(8) + sem_pair(4) + sem_pair(8) + sem_pair(3)
+        + sem_pair(8) + sem_pair(3)
+        + reduce_sems(3, 8) + reduce_sems(1, 4) + reduce_sems(1, 7),
+        compiler_params=comm_params(2),
+    )(gpart2, cot, resid, inputs, mlp_gain, mix_gain, vecs, taps_all, starts_all, start,
+      opart, dmg, dmu, dmd, wq, nall, gate_pre, lext, conv, rec, opening, state, mixed,
+      rgate_all, igate_all)
+
+
+def split_body(
+    inputs, mix_gain, gate_proj, gate_bias, lift_proj, lift_bias, conv_taps, conv_bias,
+    recur_gate, recur_bias, input_gate, input_bias, decay_param, out_proj, out_bias, mlp_gain,
+    mlp_gate, mlp_up, mlp_down, doc_starts, cotangent,
+):
+    wide = 2 * GB
+    wm = jnp.stack([gate_proj.T, lift_proj.T, out_proj])
+    vecs = jnp.stack(
+        [gate_bias, lift_bias, conv_bias, recur_bias, input_bias, jax.nn.softplus(-decay_param),
+         jax.nn.sigmoid(-decay_param), jnp.zeros_like(decay_param)]
+    ).reshape(8, 4, wide).transpose(1, 0, 2)
+    taps = conv_taps.reshape(4, 4, wide).transpose(1, 0, 2)
+    starts = jnp.pad(
+        doc_starts, ((0, 7), (0, 128 - doc_starts.shape[1])),
+        constant_values=jnp.iinfo(jnp.int32).max,
+    )
+    (wq, wg, wu, wd, nall, call, starts_all, gate_pre, lext, conv, rec, opening, state, start,
+     mixed, resid, n2all) = front(
+        inputs, cotangent, mix_gain[None], vecs, taps, recur_gate, input_gate, starts,
+        out_bias[None], mlp_gain[None], wm, mlp_gate, mlp_up, mlp_down,
+    )
+    opart, gpart2, dmg, dmu, dmd = mlp(n2all, call, wg, wu, wd)
+    output, grad_inputs, own_g, own_u, own_d, own_e, own_l, gates, gains = back(
+        gpart2, cotangent, resid, inputs, mlp_gain[None], mix_gain[None], vecs, taps, starts_all,
+        start, opart, dmg, dmu, dmd, wq, nall, gate_pre, lext, conv, rec, opening, state, mixed,
+        recur_gate, input_gate,
+    )
+    wide_out = lambda v: v.astype(F32)
+    gates = wide_out(gates).reshape(4, 2, 2, GB // 8, GB)
+    gate_out = lambda i: gates[:, i].reshape(8, GB // 8, GB)
+    own = wide_out(own_l[GB : GB + 16, :GB])
+    return (
+        output, grad_inputs, gains[0],
+        wide_out(own_e[GB:].T), own[0], wide_out(own_l[:GB].T), own[1], own[2:6], own[6],
+        gate_out(0), own[7], gate_out(1), own[8], own[9],
+        wide_out(own_e[:GB]), gains[2], gains[1],
+        wide_out(own_g), wide_out(own_u), wide_out(own_d),
+    )
+
+
 def solution(mesh):
     in_specs = (
         P(("rows", "chan"), None),
@@ -385,4 +1734,5 @@
         P(None, "chan"),
         P("chan", None),
     )
-    return jax.shard_map(body, mesh=mesh, in_specs=in_specs, out_specs=out_specs, check_vma=False)
+    split = mesh.shape["rows"] == 4 and mesh.shape["chan"] == HEADS
+    return jax.shard_map(split_body if split else body, mesh=mesh, in_specs=in_specs, out_specs=out_specs, check_vma=False)

time: 3120 us -> 347 us (0.11)
  waiting for transfers between devices: 2000 us -> 0 us
  local copies, waits for them, and re-layouts: 688 us -> 11.7 us
  Pallas kernels: 0 us -> 321 us
  other arithmetic: 153 us -> 10.4 us
  blocking collectives: 126 us -> 0 us
  matrix products: 113 us -> 0 us
    unnamed x9 -> x0, waiting for transfers between devices: 1750 us -> none
    pallas_call x0 -> x3, Pallas kernels: none -> 321 us  [the longest x1 149 us: back(): pl.pallas_call(back_kernel, name='back', out_shape=outs, in_specs=[IN_VME...]
    slice x121 -> x3, local copies, waits for them, and re-layouts: 279 us -> 2.9 us  [the longest x1 1.72 us: split_body(): gate_out = lambda i: gates[:, i].reshape(8, GB // 8, GB)]
    reshape x28 -> x0, local copies, waits for them, and re-layouts: 161 us -> none  [the longest x1 82.1 us: body(): summed = lax.psum(shared.reshape(-1), 'rows')]
    psum x1 -> x0, waiting for transfers between devices: 129 us -> none  [body(): summed = lax.psum(shared.reshape(-1), 'rows')]
    all_gather x4 -> x0, blocking collectives: 126 us -> none  [prefix(): pieces = jax.tree.map(lambda part: lax.all_gather(part, axis), value)]
    all_gather x6 -> x0, waiting for transfers between devices: 118 us -> none  [the longest x1 61.1 us: body(): lax.all_gather(gate_proj, 'chan', axis=1, tiled=True)]
    dot_general x18 -> x0, matrix products: 113 us -> none  [the longest x3 13.4 us: coefficients(): jnp.einsum('hit,hio->hot', grouped, recur_gate, precision=precise)]
  transfers between devices with their start and end apart: 10 -> 0, of which waited for: 5 -> 0; matrix products, arithmetic and copies ran while one was open for 14% -> 0% of each run, Pallas kernels for 0% -> 0%
where the time goes in v2:
time: 347 us; the launch traced here: 344 us
  Pallas kernels  321 us (93%)
  local copies, waits for them, and re-layouts  11.7 us (3%)
  other arithmetic  10.4 us (3%)
    pallas_call x1, Pallas kernels, back(): pl.pallas_call(back_kernel, name='back', out_shape=outs, in_specs=[IN_VME...  149 us
    pallas_call x1, Pallas kernels, front(): pl.pallas_call(front_kernel, name='front', out_shape=[o[0] for o in outs]...  142 us
    pallas_call x1, Pallas kernels, mlp(): pl.pallas_call(mlp_kernel, name='mlp_both_ways', grid=(blocks,), in_specs...  29.2 us
    convert_element_type x5, other arithmetic, split_body(): wide_out = lambda v: v.astype(F32)  7.29 us

profile of v2, /device:TPU:0, one launch (start us, length us, event | category | flops | bytes accessed | tf_op | source)
XLA Modules:
  0.0 343.7 jit_solution(2294303609675351356)
XLA Ops:
  0.7 1.3 pad.4.starts
  1.9 0.7 stack.36
  2.6 0.7 stack.37
  3.3 0.7 stack.38
  4.0 0.7 stack.39
  4.7 0.7 stack.40
  5.4 0.7 add_divide_fusion
  6.2 0.7 stack.43
  6.9 2.4 pad_maximum_fusion.wm
  9.3 142.3 %front.1 = (bf16[3,2,192,1024]{3,2,1,0:T(8,128)(2,1)}, bf16[2,1024,384]{2,1,0:T(8,128)(2,1)}, bf16[2,1024,384]{2,1,0:T(8,128)(2,1)}, bf16[2,384,1024]{2,1,0:T(8,...) custom-call(bf16[256,1024]{1,0:T(8,128)(2,1)} %inputs.3, ...), custom_call_target="tpu_custom_call" | custom-call | tf_op jit(solution)/shard_map/front/pallas_call | solution.py:1090
  151.6 29.2 %mlp_both_ways.1 = (bf16[4,256,1024]{2,1,0:T(8,128)(2,1)}, bf16[4,256,1024]{2,1,0:T(8,128)(2,1)}, bf16[2,1024,384]{2,1,0:T(8,128)(2,1)}, bf16[2,1024,384]{2,1,0:T(8,128)(2,1)}, bf16[2,384,1024]{2,1,0:T(8,128)(2,1)}) custom-call(bf16[4,256,1024]{2,1,0:T(8,128)(2,1)} %get-tuple-element.51.nall, bf16[4,256,1024]{2,1,0:T(8,128)(2,1)} %get-tuple-element.52.call, ...), custom_call_target="tpu_custom_call" | custom-call | tf_op jit(solution)/shard_map/mlp_both_ways/pallas_call | solution.py:1245
  180.8 149.4 %back.1 = (bf16[256,1024]{1,0:T(8,128)(2,1)}, bf16[256,1024]{1,0:T(8,128)(2,1)}, bf16[1024,384]{1,0:T(8,128)(2,1)}, bf16[1024,384]{1,0:T(8,128)(2,1)}, bf16[384,...) custom-call(bf16[4,256,1024]{2,1,0:T(8,128)(2,1)} %get-tuple-element, ...), custom_call_target="tpu_custom_call" | custom-call | tf_op jit(solution)/shard_map/back/pallas_call | solution.py:1616
  330.2 1.3 slice_bitcast_fusion
  331.5 0.7 slice_convert_fusion.1
  332.2 0.6 slice.66
  332.8 0.6 fusion.1
  333.4 1.7 fusion
  335.1 2.8 slice_convert_fusion
  337.9 1.2 convert_element_type.34
  339.3 1.2 convert_element_type.35
  340.6 0.2 copy-done
  340.8 1.3 convert_element_type.36
  342.1 0.8 copy.43
  342.9 0.8 copy.44
  (12 shorter events, 0.2 us)
Async XLA Ops:
  335.1 2.8 copy-start.2
  337.9 1.4 copy-start.1
  339.3 1.4 copy-start
  340.8 1.3 copy-start.4
  340.8 2.1 copy-start.3

commit v3 on v2

--- a/solution.py
+++ b/solution.py
@@ -621,6 +621,12 @@
     return [pltpu.SemaphoreType.DMA((pieces,))] * (5 * arrays)
 
 
+AHEAD = 4
+HOP_LAG = 3
+END_LAG = 10
+RELAY_LAG = 13
+
+
 class Reduce:
     def __init__(self, me, parts, mine, from_y, from_z, own, pieces, sems):
         self.me, self.parts, self.mine = me, parts, mine
@@ -722,39 +728,21 @@
         for copy in self.out_copies(k, self.me.core, 8):
             copy.start()
 
-    def step(self, p, ahead=2):
-        pieces = self.pieces
-        if p < 0:
-            return
-        if p < pieces:
-            self.join(p)
-            if p + ahead < pieces:
-                self.y_send(p + ahead)
-
-        def there(k):
-            return jnp.logical_and(k >= 0, k < pieces), lax.rem(k + 4 * pieces, pieces)
-
-        if p < pieces + 3:
-            inside, k = there(p - self.hop)
-
-            @pl.when(jnp.logical_and(inside, jnp.logical_not(self.owner)))
+    def step(self, q):
+        n = self.pieces
+
+        def at(k, also, action):
+            there = jnp.logical_and(k >= 0, k < n)
+
+            @pl.when(there if also is None else jnp.logical_and(there, also))
             def _():
-                self.chain(k)
-
-        if 0 <= p - 3 < pieces:
-
-            @pl.when(self.owner)
-            def _():
-                self.finish(p - 3)
-
-        if 0 <= p - 5 < pieces:
-
-            @pl.when(self.relays)
-            def _():
-                self.relay(p - 5)
-
-    def positions(self):
-        return self.pieces + 5
+                action(lax.rem(k + 8 * n, n))
+
+        at(q + AHEAD, None, self.y_send)
+        at(q, None, self.join)
+        at(q - HOP_LAG * self.hop, jnp.logical_not(self.owner), self.chain)
+        at(q - END_LAG, self.owner, self.finish)
+        at(q - RELAY_LAG, self.relays, self.relay)
 
     def close(self):
         others = jnp.logical_not(jnp.logical_or(self.owner, self.relays))
@@ -784,6 +772,42 @@
             def _():
                 for copy in self.out_copies(k, self.me.core, 8):
                     copy.wait_recv()
+
+
+class Line:
+    def __init__(self, reduces, offsets):
+        self.reduces, self.offsets, self.done = reduces, offsets, -AHEAD
+
+    def position(self, p, low, high):
+        for one, offset in zip(self.reduces, self.offsets):
+            if offset - AHEAD < high and low < offset + one.pieces + RELAY_LAG:
+                one.step(p - offset)
+
+    def advance(self, high):
+        low, self.done = self.done, high
+        if high > low + 1:
+
+            @pl.loop(low, high)
+            def _(p):
+                self.position(p, low, high)
+
+        elif high > low:
+            self.position(low, low, high)
+
+    def during(self, begin, end, action):
+        low, self.done = self.done, self.done + end - begin
+
+        @pl.loop(begin, end)
+        def _(s):
+            action(s)
+            self.position(low - begin + s, low, low + end - begin)
+
+    def last(self):
+        return self.offsets[-1] + self.reduces[-1].pieces + RELAY_LAG
+
+    def close(self):
+        for one in self.reduces:
+            one.close()
 
 
 def reduce_sems(arrays, pieces):
@@ -840,8 +864,7 @@
     ]
     for copy in heads:
         copy.start()
-    here_c = pltpu.make_async_copy(cot, call.at[r], loc.at[6])
-    here_c.start()
+    call[r] = cot[...]
     vals = inputs[...].astype(F32)
     scale = lax.rsqrt(jnp.mean(vals * vals, axis=-1, keepdims=True) + EPSILON)
     nall[r] = (vals * scale * gain[...]).astype(LOW)
@@ -850,8 +873,8 @@
 
     x_n = push(nall.at[r], nall.at[r], (xs, xr), 0, me.x)
     c_n = push(nall.at[r], nall.at[r], (cs, cr), 0, me.core)
-    c_c = push(cot, call.at[r], (cs, cr), 1, me.core)
-    x_c = push(cot, call.at[r], (xs, xr), 1, me.x)
+    c_c = push(call.at[r], call.at[r], (cs, cr), 1, me.core)
+    x_c = push(call.at[r], call.at[r], (xs, xr), 1, me.x)
     fwd_n = push(nall.at[me.r_x], nall.at[me.r_x], (cs, cr), 2, me.core)
     fwd_c = push(call.at[me.r_x], call.at[me.r_x], (cs, cr), 3, me.core)
     s_copies = [
@@ -1051,7 +1074,6 @@
         finish_sends(halo_copies)
 
     carry_sent(me, False, carry_copies)
-    here_c.wait()
     for copy in saved + [save_w] + more:
         copy.wait()
 
@@ -1069,11 +1091,11 @@
     vmem = lambda spec: pltpu.VMEM(spec.shape, spec.dtype)
     outs = [
         (sd((3, 2, wide // 2, width), LOW), ANYWHERE),
-        (sd((2, width, hidden), LOW), ANYWHERE),
-        (sd((2, width, hidden), LOW), ANYWHERE),
-        (sd((2, hidden, width), LOW), ANYWHERE),
+        (sd((2, width, hidden), LOW), IN_VMEM),
+        (sd((2, width, hidden), LOW), IN_VMEM),
+        (sd((2, hidden, width), LOW), IN_VMEM),
         (tokens, ANYWHERE),
-        (tokens, ANYWHERE),
+        (tokens, IN_VMEM),
         (sd((4,) + starts.shape, starts.dtype), IN_VMEM),
         (tall, ANYWHERE),
         (ext, ANYWHERE),
@@ -1091,7 +1113,7 @@
         front_kernel,
         name="front",
         out_shape=[o[0] for o in outs],
-        in_specs=[IN_VMEM, ANYWHERE] + [IN_VMEM] * 3 + [ANYWHERE] * 2 + [IN_VMEM] * 3 + [ANYWHERE] * 4,
+        in_specs=[IN_VMEM] * 5 + [ANYWHERE] * 2 + [IN_VMEM] * 3 + [ANYWHERE] * 4,
         out_specs=[o[1] for o in outs],
         scratch_shapes=[
             pltpu.VMEM((3, 2, wide // 2, width), LOW), vmem(tokens), pltpu.VMEM((4, 16, width), LOW),
@@ -1178,7 +1200,7 @@
     return copies
 
 
-def spread_rest(me, all_ref, first, sems_c):
+def spread_rest(me, all_ref, first, sems_c, beside=None):
     length = all_ref.shape[1]
     step = length // RS_CHUNKS
     passed = []
@@ -1188,6 +1210,8 @@
         copy = push(theirs, theirs, sems_c, RS_CHUNKS + k, me.core)
         copy.start()
         passed.append(copy)
+        if beside is not None:
+            beside(k)
     for k in range(RS_CHUNKS):
         first[k][0].wait_send()
         first[k][1].wait()
@@ -1296,19 +1320,24 @@
     for copy in loads:
         copy.start()
     greet(list(row_peers) + chan_peers)
-    n_mlp = 11 * 3
-    big = Reduce(me, [dmg, dmu, dmd], [mine_g, mine_u, mine_d], [y_g, y_u, y_d], [z_g, z_u, z_d],
-                 [own_g, own_u, own_d], 8, reduce_refs[:n_mlp])
-    mid = Reduce(me, [early], [early.at[y]], [y_e], [z_e], [own_e], 4, reduce_refs[n_mlp : n_mlp + 11])
-    end = Reduce(me, [late], [late.at[y]], [y_l], [z_l], [own_l], 7, reduce_refs[n_mlp + 11 :])
+    groups = [reduce_refs[11 * i : 11 * i + 11] for i in range(5)]
+    line = Line(
+        [
+            Reduce(me, [dmg], [mine_g], [y_g], [z_g], [own_g], 8, groups[0]),
+            Reduce(me, [dmu], [mine_u], [y_u], [z_u], [own_u], 8, groups[1]),
+            Reduce(me, [dmd], [mine_d], [y_d], [z_d], [own_d], 8, groups[2]),
+            Reduce(me, [early], [early.at[y]], [y_e], [z_e], [own_e], 8, groups[3]),
+            Reduce(me, [late], [late.at[y]], [y_l], [z_l], [own_l], 7, groups[4]),
+        ],
+        (0, 8, 16, 24, 33),
+    )
 
     copies = rows_sum_start(me, gpart2, mate, (ms, mr))
-    big.y_send(0)
-    big.y_send(1)
+    line.advance(0)
     crossing = rows_sum_cross(me, gpart2, mate, out_x, in_x, copies, (rxs, rxr))
     for copy in loads[:3]:
         copy.wait()
-    big.step(0)
+    line.advance(1)
     first = []
     gain2_sum = 0.0
     bias_sum = 0.0
@@ -1325,14 +1354,14 @@
         gresid[rows] = total
         ball[r, rows] = total.astype(LOW)
         first.append(spread_chunk(me, ball, k, (ax, bx), (ac, bc)))
-        if k % 2 == 1:
-            big.step(1 + k // 2)
+        line.advance((2, 3, 5, 6)[k])
     for copy in loads[3:]:
         copy.wait()
     pair_diagonal(rgate, rg32)
     pair_diagonal(igate, ig32)
-    big.step(3)
-    spread_rest(me, ball, first, (ac, bc))
+    line.advance(7)
+    spread_rest(me, ball, first, (ac, bc), lambda k: line.advance(9 + k))
+    o_copies = rows_sum_start(me, opart_v, o_mate, (oms, omr))
     finish_sends(copies + crossing)
 
     vec = vecs.at[r]
@@ -1376,21 +1405,15 @@
         tot[s, 0:1] = product
         tot[s, 1:2] = carried
 
-    for half in range(2):
-
-        @pl.loop(2 * half, 2 * half + 2)
-        def _(s):
-            mixer_three(s)
-
-        if half == 0:
-            big.step(4)
+    line.during(0, 4, mixer_three)
+    o_cross = rows_sum_cross(me, opart_v, o_mate, o_out, o_in, o_copies, (oxs, oxr))
 
     carry_copies = carry_start(me, True, tot, slots, (ps, pr))
     for j in range(2):
         early[j, 0:side] = acc_a[j * side : (j + 1) * side].astype(LOW)
         early[j, side : 2 * side] = acc_b[j * side : (j + 1) * side].astype(LOW)
     acc_b[...] = jnp.zeros_like(acc_b)
-    big.step(5)
+    line.advance(18)
     carry_join(me, True, slots, carry, (ps, pr))
 
     def mixer_four(s):
@@ -1425,16 +1448,7 @@
         sums[9:10] += jnp.sum(grad_log * recur, axis=0, keepdims=True) * (8.0 * vec[6:7])
         sums[6:7] += jnp.sum(total, axis=0, keepdims=True)
 
-    for half in range(2):
-
-        @pl.loop(2 * half, 2 * half + 2)
-        def _(s):
-            mixer_four(s)
-
-        if half == 0:
-            big.step(6)
-            mid.y_send(0)
-            mid.y_send(1)
+    line.during(0, 4, mixer_four)
 
     heads = [
         push(gconv.at[s, pl.ds(0, TILE)], heads_in.at[s], (hs, hr), s, (r, lax.rem(c + 7, 8)))
@@ -1463,7 +1477,7 @@
     ]
     for copy in gate_copies:
         copy.start()
-    big.step(7)
+    line.advance(24)
 
     @pl.when(c < 7)
     def _():
@@ -1489,31 +1503,20 @@
             nn(gate_low[s], wq[0].reshape(wide, width)) + nn(lift_low, wq[1].reshape(wide, width))
         ).astype(LOW)
 
-    for half in range(2):
-
-        @pl.loop(2 * half, 2 * half + 2)
-        def _(s):
-            mixer_five(s)
-
-        if half == 0:
-            big.step(8)
-            mid.step(0)
+    for k in range(RS_CHUNKS):
+        rows = pl.ds(k * step, step)
+        total = rows_sum_chunk(me, opart_v, o_mate, o_in, o_copies, o_cross, k)
+        output[rows] = (resid[rows] + total).astype(LOW)
+    line.during(0, 4, mixer_five)
 
     n_copies = rows_sum_start(me, ball, mate, (nms, nmr))
     late[...] = jnp.zeros_like(late)
     for j in range(2):
         late[j, 0:side] = acc_b[j * side : (j + 1) * side].astype(LOW)
         late[j, side : side + 16, 0:side] = sums[:, j * side : (j + 1) * side].astype(LOW)
-    end.y_send(0)
-    end.y_send(1)
-    end.y_send(2)
+    line.advance(30)
     n_cross = rows_sum_cross(me, ball, mate, out_x, in_x, n_copies, (nxs, nxr))
-    o_copies = rows_sum_start(me, opart_v, o_mate, (oms, omr))
-    o_cross = rows_sum_cross(me, opart_v, o_mate, o_out, o_in, o_copies, (oxs, oxr))
-    big.step(9)
-    mid.step(1)
-    big.step(10)
-    mid.step(2)
+    line.advance(32)
     gain_sum = 0.0
     for k in range(RS_CHUNKS):
         rows = pl.ds(k * step, step)
@@ -1526,9 +1529,7 @@
         ginputs[rows] = (
             gresid[rows] + scale * pulled - vals * (scale * scale * scale * inner)
         ).astype(LOW)
-        if k == 1:
-            big.step(11)
-            mid.step(3)
+        line.advance(33 + k)
     for k in range(8):
         lanes = slice(k * 128, (k + 1) * 128)
         gain_slots[0, k] = jnp.concatenate(
@@ -1541,17 +1542,7 @@
     ]
     for copy in gain_copies:
         copy.start()
-    big.step(12)
-    for p in range(3):
-        end.step(p, 3)
-    mid.step(4)
-    for k in range(RS_CHUNKS):
-        rows = pl.ds(k * step, step)
-        total = rows_sum_chunk(me, opart_v, o_mate, o_in, o_copies, o_cross, k)
-        output[rows] = (resid[rows] + total).astype(LOW)
-    for p in range(3, 6):
-        end.step(p, 3)
-    mid.step(5)
+    line.advance(38)
     gate_total = gate_send[c].astype(F32)
     for d in range(1, 8):
         gate_copies[d - 1].wait_recv()
@@ -1574,11 +1565,7 @@
     ]
     for copy in row_copies:
         copy.start()
-    end.step(6, 3)
-    mid.step(6)
-    for p in range(7, end.positions()):
-        end.step(p, 3)
-        mid.step(p)
+    line.advance(line.last())
     for copy in row_copies + gate_rows:
         copy.wait()
     gains_all[...] = gain_sums[0] + gain_sums[1] + gain_sums[2] + gain_sums[3]
@@ -1589,9 +1576,7 @@
 
     finish_sends(gain_copies + gate_copies + n_copies + n_cross + o_copies + o_cross)
     carry_sent(me, True, carry_copies)
-    big.close()
-    mid.close()
-    end.close()
+    line.close()
 
 
 def back(gpart2, cot, resid, inputs, mlp_gain, mix_gain, vecs, taps_all, starts_all, start,
@@ -1641,7 +1626,7 @@
         + sem_pair(RS_CHUNKS) + sem_pair(2 * RS_CHUNKS)
         + [dma((15,))] + sem_pair(8) + sem_pair(4) + sem_pair(8) + sem_pair(3)
         + sem_pair(8) + sem_pair(3)
-        + reduce_sems(3, 8) + reduce_sems(1, 4) + reduce_sems(1, 7),
+        + reduce_sems(4, 8) + reduce_sems(1, 7),
         compiler_params=comm_params(2),
     )(gpart2, cot, resid, inputs, mlp_gain, mix_gain, vecs, taps_all, starts_all, start,
       opart, dmg, dmu, dmd, wq, nall, gate_pre, lext, conv, rec, opening, state, mixed,

time: 347 us -> 284 us (0.82)
  Pallas kernels: 321 us -> 260 us
    pallas_call x1, Pallas kernels: 142 us -> 100 us  [front(): pl.pallas_call(front_kernel, name='front', out_shape=[o[0] for o in outs]...]
    pallas_call x1, Pallas kernels: 149 us -> 130 us  [back(): pl.pallas_call(back_kernel, name='back', out_shape=outs, in_specs=[IN_VME...]
where the time goes in v3:
time: 284 us; the launch traced here: 283 us
  Pallas kernels  260 us (92%)
  local copies, waits for them, and re-layouts  11.7 us (4%)
  other arithmetic  10.4 us (4%)
    pallas_call x1, Pallas kernels, back(): pl.pallas_call(back_kernel, name='back', out_shape=outs, in_specs=[IN_VME...  130 us
    pallas_call x1, Pallas kernels, front(): pl.pallas_call(front_kernel, name='front', out_shape=[o[0] for o in outs]...  100 us
    pallas_call x1, Pallas kernels, mlp(): pl.pallas_call(mlp_kernel, name='mlp_both_ways', grid=(blocks,), in_specs...  29.2 us
    convert_element_type x5, other arithmetic, split_body(): wide_out = lambda v: v.astype(F32)  7.29 us

profile of v3, /device:TPU:0, one launch (start us, length us, event | category | flops | bytes accessed | tf_op | source)
XLA Modules:
  0.0 282.5 jit_solution(11020272718178008255)
XLA Ops:
  0.7 1.3 pad.4.starts
  1.9 0.7 stack.36
  2.6 0.7 stack.37
  3.3 0.7 stack.38
  4.0 0.7 stack.39
  4.7 0.7 stack.40
  5.4 0.7 add_divide_fusion
  6.2 0.7 stack.43
  6.9 2.4 pad_maximum_fusion.wm
  9.3 100.2 %front.1 = (bf16[3,2,192,1024]{3,2,1,0:T(8,128)(2,1)}, bf16[2,1024,384]{2,1,0:T(8,128)(2,1)}, bf16[2,1024,384]{2,1,0:T(8,128)(2,1)}, bf16[2,384,1024]{2,1,0:T(8,...) custom-call(bf16[256,1024]{1,0:T(8,128)(2,1)} %inputs.3, ...), custom_call_target="tpu_custom_call" | custom-call | tf_op jit(solution)/shard_map/front/pallas_call | solution.py:1112
  109.5 29.2 %mlp_both_ways.1 = (bf16[4,256,1024]{2,1,0:T(8,128)(2,1)}, bf16[4,256,1024]{2,1,0:T(8,128)(2,1)}, bf16[2,1024,384]{2,1,0:T(8,128)(2,1)}, bf16[2,1024,384]{2,1,0:T(8,128)(2,1)}, bf16[2,384,1024]{2,1,0:T(8,128)(2,1)}) custom-call(bf16[4,256,1024]{2,1,0:T(8,128)(2,1)} %get-tuple-element.51.nall, bf16[4,256,1024]{2,1,0:T(8,128)(2,1)} %get-tuple-element.52.call, ...), custom_call_target="tpu_custom_call" | custom-call | tf_op jit(solution)/shard_map/mlp_both_ways/pallas_call | solution.py:1269
  138.7 130.3 %back.1 = (bf16[256,1024]{1,0:T(8,128)(2,1)}, bf16[256,1024]{1,0:T(8,128)(2,1)}, bf16[1024,384]{1,0:T(8,128)(2,1)}, bf16[1024,384]{1,0:T(8,128)(2,1)}, bf16[384,...) custom-call(bf16[4,256,1024]{2,1,0:T(8,128)(2,1)} %get-tuple-element, ...), custom_call_target="tpu_custom_call" | custom-call | tf_op jit(solution)/shard_map/back/pallas_call | solution.py:1601
  269.0 1.3 slice_bitcast_fusion
  270.4 0.7 slice_convert_fusion.1
  271.1 0.6 slice.66
  271.7 0.6 fusion.1
  272.2 1.7 fusion
  274.0 2.8 slice_convert_fusion
  276.8 1.2 convert_element_type.34
  278.2 1.2 convert_element_type.35
  279.4 0.2 copy-done
  279.6 1.3 convert_element_type.36
  280.9 0.8 copy.43
  281.7 0.8 copy.44
  (12 shorter events, 0.2 us)
Async XLA Ops:
  274.0 2.8 copy-start.2
  276.8 1.4 copy-start.1
  278.2 1.4 copy-start
  279.6 1.3 copy-start.4
  279.6 2.1 copy-start.3
